TPU v7x, 128 devices: a whole 4x4x4 slice. The times are simulated.
128 devices in a mesh: tm: 4 (over z), det: 32 (over y, x, core).
Axes of the slice: x: 4, y: 4, z: 4, core: 2. Of those that a mesh axis runs over, the one named last changes fastest.
Arguments:
- time_stream: bfloat16 [1024, 131072], P('det', 'tm'), may hold values from -6 to 6
- filter_taps: bfloat16 [1024, 129], P('det'), may hold values from -0.5 to 0.5
- det_precision: bfloat16 [1024, 1024], replicated
- left_weight: float32 [128, 32], replicated, may hold values from -0.046875 to 0.046875
- right_weight: float32 [128, 32], replicated, may hold values from -1 to 1
- frame_tile: int32 [131072, 1], P(('tm', 'det')), may hold values from 0 to 255; in each aligned block of 1024 rows (0 to 1023, 1024 to 2047, ...) at most 6 rows name the same one
- tile_owner: int32 [256], replicated, may hold values from 0 to 127, as said below
- frame_count: int32 [128], P(('tm', 'det')), may hold values from 512 to 1024, as said below
Outputs:
- sky_map: float32 [256, 16384], P(('tm', 'det'))
Inputs may be any that keep to these rules, and one draw needn't show every extreme that they name: `frame_tile`: within the frames of one segment (aligned blocks of 1024 rows) no tile is named more than 6 times, a bound that some block reaches. `tile_owner`: every device number is the owner of exactly 2 tiles. `frame_count`: some segment has all 1024 frames live.
All inputs are finite; a program needn't handle non-finite values.
Results may differ from a plain program's by a relative error of at most 0.0041.
Values may be sent and summed in bfloat16 or wider, within the bound.
No kernel may reach another device: no remote copies, remote signals or barrier semaphores. Data moves between devices by JAX's collectives and lax.ppermute only.
A program may use at most 64 MiB of HBM per device.

v0:
```python
import jax
import jax.numpy as jnp
from jax import lax
from jax.sharding import PartitionSpec as P

HW = 64
TILE_DEV = 2


def with_halo(block, sides, width):
    for axis, dim in sides:
        count = lax.axis_size(axis)
        forward = [(i, i + 1) for i in range(count - 1)]
        backward = [(target, source) for source, target in forward]
        low = lax.ppermute(
            lax.slice_in_dim(block, block.shape[dim] - width, None, axis=dim), axis, forward
        )
        high = lax.ppermute(lax.slice_in_dim(block, 0, width, axis=dim), axis, backward)
        block = jnp.concatenate([low, block, high], axis=dim)
    return block


def toeplitz_rows(filter_taps, half_width):
    detectors = filter_taps.shape[0]
    taps_count = filter_taps.shape[1]
    length = 4 * half_width + 1
    widened = jnp.pad(filter_taps, ((0, 0), (0, length - taps_count)))
    tiled = jnp.broadcast_to(widened[:, None, :], (detectors, 2 * half_width, length)).reshape(
        detectors, 2 * half_width * length
    )
    return tiled[:, : 2 * half_width * 4 * half_width].reshape(
        detectors, 2 * half_width, 4 * half_width
    )


def apply_filter(padded, filter_taps, half_width):
    detectors = padded.shape[0]
    blocks = (padded.shape[1] - 2 * half_width) // (2 * half_width)
    pieces = padded.reshape(detectors, blocks + 1, 2 * half_width)
    matrix = toeplitz_rows(filter_taps, half_width)
    lower = jnp.einsum(
        "dbj,dij->dbi", pieces, matrix[:, :, : 2 * half_width], preferred_element_type=jnp.float32
    )
    upper = jnp.einsum(
        "dbj,dij->dbi", pieces, matrix[:, :, 2 * half_width :], preferred_element_type=jnp.float32
    )
    result = lower[:, :-1] + upper[:, 1:]
    return result.reshape(detectors, blocks * 2 * half_width)


def owner_rows(tile_owner):
    total_tiles = tile_owner.shape[0]
    same_owner = tile_owner[:, None] == tile_owner[None, :]
    earlier = jnp.arange(total_tiles)[None, :] < jnp.arange(total_tiles)[:, None]
    slot_rank = jnp.sum((same_owner & earlier).astype(jnp.int32), axis=1)
    return tile_owner * TILE_DEV + slot_rank


def project(summed, left_weight, right_weight):
    tiles_here = summed.shape[0]
    frame_cube = summed.reshape(tiles_here, left_weight.shape[1], right_weight.shape[1])
    partial_value = jnp.einsum(
        "naf,jf->naj", frame_cube, right_weight, precision=lax.Precision.HIGHEST
    )
    result = jnp.einsum("ia,naj->nij", left_weight, partial_value, precision=lax.Precision.HIGHEST)
    return result.reshape(tiles_here, left_weight.shape[0] * right_weight.shape[0])


def local(
    time_stream,
    filter_taps,
    det_precision,
    left_weight,
    right_weight,
    frame_tile,
    tile_owner,
    frame_count,
):
    padded = with_halo(time_stream, (("tm", 1),), HW)
    filtered = apply_filter(padded, filter_taps, HW).astype(jnp.bfloat16)
    regrouped = lax.all_to_all(filtered, "det", split_axis=1, concat_axis=0, tiled=True)
    frame_height = left_weight.shape[1]
    frame_length = right_weight.shape[1]
    detectors_all = det_precision.shape[0]
    groups = detectors_all // frame_height
    columns = regrouped.shape[1] // frame_length
    precision_rows = det_precision.reshape(groups, frame_height, detectors_all)
    sample_rows = regrouped.reshape(detectors_all, columns, frame_length)
    frame_cube = jnp.einsum(
        "gak,kcf->gcaf", precision_rows, sample_rows, preferred_element_type=jnp.float32
    ).astype(jnp.bfloat16)
    frames_here = groups * columns
    frame_width = frame_height * frame_length
    frame_matrix = frame_cube.reshape(frames_here, frame_width)
    tiles_all = tile_owner.shape[0]
    capacity = max(2, 3 * frames_here // (2 * tiles_all))
    tile_index = jnp.arange(tiles_all, dtype=jnp.int32)
    alive_mask = jnp.arange(frames_here, dtype=jnp.int32) < frame_count[0]
    on_tile = frame_tile[:, 0][:, None] == tile_index[None, :]
    dest_row = jnp.sum(jnp.where(on_tile, owner_rows(tile_owner)[None, :], 0), axis=1)
    live_hits = (on_tile & alive_mask[:, None]).astype(jnp.int32)
    earlier = jnp.cumsum(live_hits, axis=0) - live_hits
    slot_rank = jnp.sum(jnp.where(on_tile, earlier, 0), axis=1)
    position = jnp.where(alive_mask, dest_row * capacity + slot_rank, tiles_all * capacity)
    slot_ids = jnp.arange(tiles_all * capacity, dtype=jnp.int32)
    placing = (slot_ids[:, None] == position[None, :]).astype(jnp.bfloat16)
    placed = jnp.dot(placing, frame_matrix, preferred_element_type=jnp.float32)
    buffer = placed.astype(jnp.bfloat16).reshape(
        tiles_all // TILE_DEV, TILE_DEV, capacity * frame_width
    )
    received = lax.all_to_all(buffer, ("tm", "det"), split_axis=0, concat_axis=0, tiled=True)
    summed = jnp.sum(
        received.reshape(received.shape[0], received.shape[1], capacity, frame_width),
        axis=(0, 2),
        dtype=jnp.float32,
    )
    return project(summed, left_weight, right_weight)


def solution(mesh):
    return jax.shard_map(
        local,
        mesh=mesh,
        in_specs=(
            P("det", "tm"),
            P("det", None),
            P(),
            P(),
            P(),
            P(("tm", "det"), None),
            P(),
            P(("tm", "det")),
        ),
        out_specs=P(("tm", "det"), None),
        check_vma=False,
    )
```

profile of v0, /device:TPU:1, one launch (start us, length us, event | category | flops | bytes accessed | tf_op | source)
XLA Modules:
  0.0 229.5 jit_solution(3069472556426601585)
XLA Ops:
  0.0 0.9 fusion.25
  0.9 4.4 %collective-permute-start = (bf16[32,64]{1,0:T(8,128)(2,1)S(1)}, bf16[32,64]{1,0:T(8,128)(2,1)S(1)}, u32[]{:S(2)}, u32[]{:S(2)}) collective-permute-start(bf16[32,64]{1,0:T(8,128)(2,1)S(1)} %get-tuple-element.8), channel_id=1, source_target_pairs={{0,32},{32,64},{64,96},{1,33},{33,65},{65,97},{2,34},{34,66},{66,9... | collective-permute-start | bytes 12296 | tf_op jit(solution)/shard_map/ppermute | solution.py:15
  5.3 1.3 collective-permute-start.1
  6.6 0.7 pad.4
  7.3 1.9 broadcast_in_dim.23
  9.3 6.2 %reshape.79 = bf16[32,32896]{1,0:T(8,128)(2,1)} reshape(bf16[32,128,257]{2,1,0:T(8,128)(2,1)} %broadcast_in_dim.23) | data formatting | bytes 4210688 | tf_op jit(solution)/shard_map/reshape | solution.py:28
  15.5 1.6 slice-done
  17.1 1.9 copy.26
  18.9 1.3 dynamic-update-slice
  20.3 13.9 %dynamic-update-slice.1 = bf16[32,32896]{1,0:T(8,128)(2,1)} dynamic-update-slice(bf16[32,32896]{1,0:T(8,128)(2,1)} %dynamic-update-slice, bf16[32,32768]{1,0:T(8,128)(2,1)} %param.8, s32[]{} %constant.20, s32[]{} %constant.21) | dynamic-update-slice | bytes 4194308
  34.1 1.4 dynamic-update-slice.2
  35.5 4.2 %reshape.78 = bf16[32,257,128]{2,1,0:T(8,128)(2,1)} reshape(bf16[32,32896]{1,0:T(8,128)(2,1)} %dynamic-update-slice.2) | data formatting | bytes 4210688 | tf_op jit(solution)/shard_map/reshape | solution.py:39
  39.7 2.7 %fusion.7 = f32[32,256,128]{2,1,0:T(8,128)S(1)} fusion(bf16[32,257,128]{2,1,0:T(8,128)(2,1)} %reshape.78, bf16[32,128,256]{2,1,0:T(8,128)(2,1)} %bitcast.46), kind=kOutput, calls=%fused_computation.9 | convolution fusion | flops 268435456 | bytes 7340032 | tf_op jit(solution)/shard_map/dbj,dij->dbi/dot_general | solution.py:44
  42.5 0.5 copy-done.3
  42.9 2.0 add_convert_fusion
  44.9 4.2 %convert_element_type.37 = bf16[32,32,1024]{2,1,0:T(8,128)(2,1)} reshape(bf16[32,256,128]{2,1,0:T(8,128)(2,1)} %add_convert_fusion) | data formatting | bytes 4194304 | tf_op jit(solution)/shard_map/convert_element_type | solution.py:80
  49.1 4.0 %copy.19 = bf16[32,32,1024]{2,0,1:T(8,128)(2,1)} copy(bf16[32,32,1024]{2,1,0:T(8,128)(2,1)} %convert_element_type.37) | data formatting | bytes 4194304 | tf_op jit(solution)/shard_map/convert_element_type | solution.py:80
  53.1 8.2 %all-to-all-start = ((bf16[32,32,1024]{2,0,1:T(8,128)(2,1)}), bf16[32,32,1024]{2,0,1:T(8,128)(2,1)}, u32[]{:S(2)}, u32[]{:S(2)}) async-start(bf16[32,32,1024]{2,0,1:T(8,128)(2,1)} %copy.19), calls=%async_computation | async-start | bytes 4194304 | tf_op jit(solution)/shard_map/all_to_all | solution.py:81
  62.2 0.3 fusion.14
  62.7 0.3 copy.18
  63.4 1.2 select_reduce_fusion
  64.6 24.6 %all-to-all-done = bf16[32,32,1024]{2,0,1:T(8,128)(2,1)} async-done(((bf16[32,32,1024]{2,0,1:T(8,128)(2,1)}), bf16[32,32,1024]{2,0,1:T(8,128)(2,1)}, u32[]{:S(2)}, u32[]{:S(2)}) %all-to-all-start) | async-done | bytes 2097184 | tf_op jit(solution)/shard_map/all_to_all | solution.py:81
  89.2 10.9 %reshape.81 = bf16[1024,32,32]{2,1,0:T(8,128)(2,1)} reshape(bf16[32,32,1024]{2,1,0:T(8,128)(2,1)} %bitcast.6) | data formatting | bytes 4194304 | tf_op jit(solution)/shard_map/reshape | solution.py:88
  100.1 38.6 %convert_bitcast_fusion = bf16[32,32,32,32]{2,3,0,1:T(8,128)(2,1)} fusion(bf16[32,32,1024,1]{2,1,0,3:T(8,128)(2,1)S(1)} %bitcast.43, bf16[1024,32,32,1]{2,1,0,3:T(8,128)(2,1)} %bitcast.45), kind=kOutput, calls=%fused_computation.2 | convolution fusion | flops 2148532224 | bytes 6291456 | tf_op jit(solution)/shard_map/gak,kcf->gcaf/dot_general | solution.py:89
  138.7 12.0 %copy.21 = bf16[32,32,32,32]{3,2,1,0:T(8,128)(2,1)} copy(bf16[32,32,32,32]{2,3,0,1:T(8,128)(2,1)} %convert_bitcast_fusion) | data formatting | bytes 4194304 | tf_op jit(solution)/shard_map/convert_element_type | solution.py:91
  150.7 11.3 %reshape.83 = bf16[1024,1024]{1,0:T(8,128)(2,1)S(1)} reshape(bf16[32,32,32,32]{3,2,1,0:T(8,128)(2,1)} %copy.21) | data formatting | bytes 4194304 | tf_op jit(solution)/shard_map/reshape | solution.py:94
  162.0 5.0 %fusion.5 = bf16[1536,1024]{1,0:T(8,128)(2,1)} fusion(bf16[1024,1024]{1,0:T(8,128)(2,1)S(1)} %reshape.83, s32[1024]{0:T(1024)S(1)} %add_select_fusion), kind=kOutput, calls=%fused_computation.7 | convolution fusion | flops 3224371200 | bytes 5246976 | tf_op jit(solution)/shard_map/dot_general | solution.py:107
  167.0 8.0 %reshape.84 = bf16[128,2,6144]{2,1,0:T(2,128)(2,1)} reshape(bf16[1536,1024]{1,0:T(8,128)(2,1)} %fusion.5) | data formatting | bytes 6291456 | tf_op jit(solution)/shard_map/reshape | solution.py:108
  175.0 50.3 %all_to_all.18 = bf16[128,2,6144]{2,1,0:T(2,128)(2,1)S(1)} all-to-all(bf16[128,2,6144]{2,1,0:T(2,128)(2,1)} %reshape.84), channel_id=1, replica_groups=mesh['tm'=4,'det'=32] {'tm','det'}, dimensions={0} | all-to-all | bytes 6291456 | tf_op jit(solution)/shard_map/all_to_all | solution.py:111
  225.3 2.5 %convert_reduce_fusion = f32[2,6144]{1,0:T(2,128)S(1)} fusion(bf16[128,2,6144]{2,1,0:T(2,128)(2,1)S(1)} %all_to_all.18), kind=kLoop, calls=%fused_computation.3 | loop fusion | flops 3133440 | bytes 3194880 | tf_op jit(solution)/shard_map/reduce_sum | solution.py:112
  228.2 0.4 convolution_bitcast_fusion
  228.7 0.8 copy.33
  (34 shorter events, 1.1 us)
Async XLA Ops:
  0.0 100.1 %copy-start = (bf16[1024,1024]{1,0:T(8,128)(2,1)S(1)}, bf16[1024,1024]{1,0:T(8,128)(2,1)}, u32[]{:S(2)}) copy-start(bf16[1024,1024]{1,0:T(8,128)(2,1)} %param.10) | copy-start | bytes 6291460
  0.9 18.0 %collective-permute-start = (bf16[32,64]{1,0:T(8,128)(2,1)S(1)}, bf16[32,64]{1,0:T(8,128)(2,1)S(1)}, u32[]{:S(2)}, u32[]{:S(2)}) collective-permute-start(bf16[32,64]{1,0:T(8,128)(2,1)S(1)} %get-tuple-element.8), channel_id=1, source_target_pairs={{0,32},{32,64},{64,96},{1,33},{33,65},{65,97},{2,34},{34,66},{66,9... | collective-permute-start | bytes 12296 | tf_op jit(solution)/shard_map/ppermute | solution.py:15
  5.3 28.8 %collective-permute-start.1 = (bf16[32,64]{1,0:T(8,128)(2,1)S(1)}, bf16[32,64]{1,0:T(8,128)(2,1)S(1)}, u32[]{:S(2)}, u32[]{:S(2)}) collective-permute-start(bf16[32,64]{1,0:T(8,128)(2,1)S(1)} %get-tuple-element.7), channel_id=1, source_target_pairs={{32,0},{64,32},{96,64},{33,1},{65,33},{97,65},{34,2},{66,34},{98,6... | collective-permute-start | bytes 12296 | tf_op jit(solution)/shard_map/ppermute | solution.py:18
  15.5 1.6 slice-start
  39.7 2.7 %copy-start.2 = (bf16[32,257,128]{2,1,0:T(8,128)(2,1)S(1)}, bf16[32,257,128]{2,1,0:T(8,128)(2,1)}, u32[]{:S(2)}) copy-start(bf16[32,257,128]{2,1,0:T(8,128)(2,1)} %reshape.78) | copy-start | bytes 6316036
  39.7 3.2 %copy-start.3 = (bf16[4,8,128,256]{3,2,1,0:T(8,128)(2,1)S(1)}, bf16[4,8,128,256]{3,2,1,0:T(8,128)(2,1)}, u32[]{:S(2)}) copy-start(bf16[4,8,128,256]{3,2,1,0:T(8,128)(2,1)} %copy.26) | copy-start | bytes 6291460
  53.1 8.9 %copy-start.4 = (s32[1024,1]{0,1:T(1,128)S(1)}, s32[1024,1]{0,1:T(1,128)}, u32[]{:S(2)}) copy-start(s32[1024,1]{0,1:T(1,128)} %param.13) | copy-start | bytes 12292
  53.1 36.0 %all-to-all-start = ((bf16[32,32,1024]{2,0,1:T(8,128)(2,1)}), bf16[32,32,1024]{2,0,1:T(8,128)(2,1)}, u32[]{:S(2)}, u32[]{:S(2)}) async-start(bf16[32,32,1024]{2,0,1:T(8,128)(2,1)} %copy.19), calls=%async_computation | async-start | bytes 4194304 | tf_op jit(solution)/shard_map/all_to_all | solution.py:81
  62.6 0.7 copy-start.7
  175.0 54.5 %copy-start.1 = (bf16[1024,1024]{1,0:T(8,128)(2,1)S(1)}, bf16[1024,1024]{1,0:T(8,128)(2,1)}, u32[]{:S(2)}) copy-start(bf16[1024,1024]{1,0:T(8,128)(2,1)} %param.10) | copy-start | bytes 6291460
  225.3 2.7 %copy-start.5 = (f32[128,32]{0,1:T(8,128)S(1)}, f32[128,32]{0,1:T(8,128)}, u32[]{:S(2)}) copy-start(f32[128,32]{0,1:T(8,128)} %param.12) | copy-start | bytes 49156
  225.3 2.9 %copy-start.6 = (f32[128,32]{0,1:T(8,128)S(1)}, f32[128,32]{0,1:T(8,128)}, u32[]{:S(2)}) copy-start(f32[128,32]{0,1:T(8,128)} %param.11) | copy-start | bytes 49156
where the time goes:
time: 231 us; the launch traced here: 229 us
  local copies, waits for them, and re-layouts  86.6 us (37%)
  blocking collectives  50.3 us (22%)
  matrix products  48.9 us (21%)
  waiting for transfers between devices  24.6 us (11%)
  starting transfers between devices  13.9 us (6%)
  other arithmetic  4.36 us (2%)
    all_to_all x1, blocking collectives, local(): lax.all_to_all(buffer, ('tm', 'det'), split_axis=0, concat_axis=0, tiled=...  50.3 us
    dot_general x1, matrix products, local(): jnp.einsum('gak,kcf->gcaf', precision_rows, sample_rows, preferred_elemen...  38.6 us
    all_to_all x1, waiting for transfers between devices, local(): lax.all_to_all(filtered, 'det', split_axis=1, concat_axis=0, tiled=True)  24.6 us
    unnamed x20, local copies, waits for them, and re-layouts  18.5 us
    convert_element_type x1, local copies, waits for them, and re-layouts, local(): frame_cube = jnp.einsum('gak,kcf->gcaf', precision_rows, sample_rows, pre...  12 us
    reshape x1, local copies, waits for them, and re-layouts, local(): frame_matrix = frame_cube.reshape(frames_here, frame_width)  11.3 us
    reshape x1, local copies, waits for them, and re-layouts, local(): sample_rows = regrouped.reshape(detectors_all, columns, frame_length)  10.9 us
    all_to_all x1, starting transfers between devices, local(): lax.all_to_all(filtered, 'det', split_axis=1, concat_axis=0, tiled=True)  8.24 us
  transfers between devices with their start and end apart: 3, of which 1 were waited for; matrix products, arithmetic and copies ran while one was open for 12% of the time, Pallas kernels for 0%

commit v1 on v0

v1 whole, which is shorter than its diff:
```python
import functools

import jax
import jax.numpy as jnp
from jax import lax
from jax.experimental import pallas as pl
from jax.experimental.pallas import tpu as pltpu
from jax.sharding import PartitionSpec as P

F32 = jnp.float32
BF16 = jnp.bfloat16
ANY_NT = (((1,), (1,)), ((), ()))
TN = (((0,), (0,)), ((), ()))


def iota(shape, dim):
    return lax.broadcasted_iota(jnp.int32, shape, dim)


def params(mib):
    return pltpu.CompilerParams(vmem_limit_bytes=mib << 20)


def list_kernel(count_ref, tile_ref, owner_ref, out_ref):
    owner = owner_ref[...]
    row, col = iota((256, 256), 0), iota((256, 256), 1)
    owner_col = jnp.sum(jnp.where(row == col, owner, 0), axis=1, keepdims=True)
    rank = jnp.sum(jnp.where((owner_col == owner) & (col < row), 1, 0), axis=1, keepdims=True)
    dest_col = owner_col * 2 + rank
    number = iota((256, 128), 0)
    count = count_ref[0]
    rows = []
    for r in range(8):
        tile = tile_ref[r : r + 1, :]
        dest = jnp.sum(jnp.where(number == tile, dest_col, 0), axis=0, keepdims=True)
        rows.append(jnp.where(iota((1, 128), 1) + r * 128 < count, dest, 256))
    natural = jnp.concatenate(rows, axis=0).astype(F32).astype(BF16)
    lane, place = iota((128, 1024), 0), iota((128, 1024), 1)
    wanted = ((place % 16) // 4) * 32 + (place // 128) * 4 + place % 4
    spread = jnp.dot(natural, jnp.where(lane == wanted, 1.0, 0.0).astype(BF16), preferred_element_type=F32)
    mine = iota((8, 128), 0) == iota((8, 128), 1) // 16
    picked = [
        jnp.sum(jnp.where(mine, spread[:, c * 128 : (c + 1) * 128], 0.0), axis=0, keepdims=True)
        for c in range(8)
    ]
    out_ref[...] = jnp.broadcast_to(jnp.concatenate(picked, axis=0)[None], out_ref.shape)


def butterfly(arrays, chunk):
    lane = iota(arrays[0].shape, 1)
    for bit in range(4):
        step = 1 << bit
        low = (lane // (chunk * step)) % 2 == 0
        for i in range(16):
            if i & step:
                continue
            a, b = arrays[i], arrays[i + step]
            arrays[i] = jnp.where(low, a, pltpu.roll(b, chunk * step, 1))
            arrays[i + step] = jnp.where(low, pltpu.roll(a, 128 - chunk * step, 1), b)
    return arrays


def filter_kernel(x_ref, low_ref, high_ref, taps_ref, precision_ref, b_ref, rep_ref, rows_ref, y_ref):
    me = lax.axis_index("det")
    chosen = jnp.where(iota((1024, 256), 0) - me * 32 == iota((1024, 256), 1) // 8, 1.0, 0.0).astype(BF16)
    rep_ref[...] = jnp.dot(precision_ref[...], chosen, preferred_element_type=F32).astype(BF16)
    first_half = iota((256, 128), 1) < 64
    for half in range(2):
        for g in range(2):
            dg = half * 2 + g
            rows_ref[0:8, :] = low_ref[dg].astype(F32)
            rows_ref[8 + 2048 : 16 + 2048, :] = high_ref[dg].astype(F32)
            rows_ref[8 : 8 + 2048, :] = x_ref[dg].astype(F32).reshape(2048, 128)
            for d in range(8):
                before = rows_ref[pl.ds(d, 256, stride=8), :]
                here = rows_ref[pl.ds(8 + d, 256, stride=8), :]
                after = rows_ref[pl.ds(16 + d, 256, stride=8), :]
                window = jnp.concatenate([here, jnp.where(first_half, after, before)], axis=1).astype(BF16)
                taps = jnp.broadcast_to(taps_ref[dg * 8 + d : dg * 8 + d + 1, :], (128, 256))
                matrix = pltpu.roll(taps, 192, 1, stride=1, stride_axis=0).astype(BF16)
                y_ref[g * 8 + d] = lax.dot_general(window, matrix, ANY_NT, preferred_element_type=F32)

        def chunk(i, carry):
            at = pl.multiple_of(i * 16, 16)
            out = butterfly([y_ref[e, pl.ds(at, 16), :] for e in range(16)], 8)
            for q in range(16):
                lanes = (q % 4) * 256 + half * 128
                b_ref[pl.ds(pl.multiple_of((q // 4) * 256 + at, 16), 16), lanes : lanes + 128] = out[q].astype(BF16)
            return carry

        lax.fori_loop(0, 16, chunk, 0)


def sum_kernel(list_ref, b_ref, rep_ref, out_ref, lists_ref, hot_ref, w_ref, acc_ref, rows_ref):
    lists_ref[...] = list_ref[...].T
    number = iota((256, 256), 0).astype(F32)
    acc_ref[...] = jnp.zeros_like(acc_ref)

    def group(i, carry):
        for g in range(4):
            for c in range(4):
                names = lists_ref[pl.ds(i * 16 + g * 4 + c, 1), :]
                hot_ref[g * 256 : (g + 1) * 256, c * 256 : (c + 1) * 256] = jnp.where(number == names, 1.0, 0.0).astype(BF16)
            rep = rep_ref[pl.ds(pl.multiple_of(i * 128 + g * 32, 32), 32), :]
            for f in range(8):
                w_ref[f * 32 : (f + 1) * 32, g * 256 : (g + 1) * 256] = jnp.where(
                    iota((32, 256), 1) % 8 == f, rep.astype(F32), 0.0
                ).astype(BF16)
        for n in range(4):
            cols = slice(n * 256, (n + 1) * 256)
            s = jnp.dot(hot_ref[...], b_ref[:, cols], preferred_element_type=F32).astype(BF16)
            wide = jnp.concatenate([s[g * 256 : (g + 1) * 256] for g in range(4)], axis=1)
            acc_ref[:, cols] += lax.dot_general(wide, w_ref[...], ANY_NT, preferred_element_type=F32)
        return carry

    lax.fori_loop(0, 8, group, 0)
    for t in range(8):
        rows_ref[pl.ds(t, 256, stride=8), :] = acc_ref[:, t * 128 : (t + 1) * 128]
    out_ref[...] = rows_ref[...].astype(BF16).reshape(out_ref.shape)


def tile_kernel(in_ref, left_ref, right_ref, out_ref):
    total = jnp.sum(in_ref[...].astype(F32), axis=0)
    left = left_ref[...]
    wide = jnp.concatenate([left] * 4, axis=0)
    lane_group = iota((128, 128), 0) // 32
    for t in range(2):
        frame = total[t * 8 : (t + 1) * 8]
        parts = [
            jnp.dot(
                frame,
                jnp.where(lane_group == q, wide, 0.0),
                precision=lax.Precision.HIGHEST,
                preferred_element_type=F32,
            )
            for q in range(4)
        ]
        mixed = jnp.concatenate(parts, axis=0)
        tile = lax.dot_general(
            mixed, right_ref[...], TN, precision=lax.Precision.HIGHEST, preferred_element_type=F32
        )
        out_ref[pl.ds(t, 128, stride=2), :] = tile


def vmem(n):
    return [pl.BlockSpec(memory_space=pltpu.VMEM)] * n


def make_list(frame_count, tiles, owner):
    return pl.pallas_call(
        list_kernel,
        out_shape=jax.ShapeDtypeStruct((32, 8, 128), F32),
        in_specs=[pl.BlockSpec(memory_space=pltpu.SMEM)] + vmem(2),
        out_specs=vmem(1)[0],
        compiler_params=params(16),
        cost_estimate=pl.CostEstimate(flops=4_000_000, bytes_accessed=200_000, transcendentals=0),
        name="make_list",
    )(frame_count, tiles, owner)


def make_filtered(x, low, high, taps, precision):
    return pl.pallas_call(
        filter_kernel,
        out_shape=(jax.ShapeDtypeStruct((1024, 1024), BF16), jax.ShapeDtypeStruct((1024, 256), BF16)),
        in_specs=vmem(5),
        out_specs=tuple(vmem(2)),
        scratch_shapes=[pltpu.VMEM((2064, 128), F32), pltpu.VMEM((16, 256, 128), F32)],
        compiler_params=params(40),
        cost_estimate=pl.CostEstimate(flops=5_000_000_000, bytes_accessed=7_000_000, transcendentals=0),
        name="make_filtered",
    )(x, low, high, taps, precision)


def make_sums(lists, filtered, rep):
    return pl.pallas_call(
        sum_kernel,
        out_shape=jax.ShapeDtypeStruct((128, 16, 128), BF16),
        in_specs=vmem(3),
        out_specs=vmem(1)[0],
        scratch_shapes=[
            pltpu.VMEM((128, 256), F32),
            pltpu.VMEM((1024, 1024), BF16),
            pltpu.VMEM((256, 1024), BF16),
            pltpu.VMEM((256, 1024), F32),
            pltpu.VMEM((2048, 128), F32),
        ],
        compiler_params=params(40),
        cost_estimate=pl.CostEstimate(flops=22_000_000_000, bytes_accessed=3_000_000, transcendentals=0),
        name="make_sums",
    )(lists, filtered, rep)


def make_tiles(received, left, right):
    return pl.pallas_call(
        tile_kernel,
        out_shape=jax.ShapeDtypeStruct((256, 128), F32),
        in_specs=vmem(3),
        out_specs=vmem(1)[0],
        compiler_params=params(16),
        cost_estimate=pl.CostEstimate(flops=40_000_000, bytes_accessed=700_000, transcendentals=0),
        name="make_tiles",
    )(received, left, right)


def split_rows(a):
    return a.reshape(4, 8, -1, 128).transpose(0, 2, 1, 3)


def local(time_stream, filter_taps, det_precision, left_weight, right_weight, frame_tile, tile_owner, frame_count):
    count = lax.axis_size("tm")
    forward = [(i, i + 1) for i in range(count - 1)]
    backward = [(j, i) for i, j in forward]
    low = lax.ppermute(time_stream[:, -128:], "tm", forward)
    high = lax.ppermute(time_stream[:, :128], "tm", backward)
    own = make_list(frame_count, frame_tile.reshape(8, 128), tile_owner.reshape(1, 256))
    lists = lax.all_to_all(own, "det", split_axis=0, concat_axis=0, tiled=True)
    taps = jnp.pad(filter_taps.astype(F32), ((0, 0), (0, 256 - filter_taps.shape[1])))
    filtered, rep = make_filtered(
        split_rows(time_stream), low.reshape(4, 8, 128), high.reshape(4, 8, 128), taps, det_precision
    )
    sums = make_sums(lists.reshape(256, 128), filtered, rep)
    received = lax.all_to_all(sums, ("tm", "det"), split_axis=0, concat_axis=0, tiled=True)
    right = right_weight.reshape(128, 8, 4).transpose(2, 1, 0).reshape(32, 128)
    tiles = make_tiles(received, left_weight.T, right)
    return tiles.reshape(128, 2, 128).transpose(1, 0, 2).reshape(2, 16384)


def solution(mesh):
    return jax.shard_map(
        local,
        mesh=mesh,
        in_specs=(
            P("det", "tm"),
            P("det", None),
            P(),
            P(),
            P(),
            P(("tm", "det"), None),
            P(),
            P(("tm", "det")),
        ),
        out_specs=P(("tm", "det"), None),
        check_vma=False,
    )
```

time: 231 us -> 103 us (0.45)
  local copies, waits for them, and re-layouts: 86.6 us -> 5.27 us
  Pallas kernels: 0 us -> 57 us
  blocking collectives: 50.3 us -> 0 us
  matrix products: 48.9 us -> 0 us
  waiting for transfers between devices: 24.6 us -> 13.7 us
  starting transfers between devices: 13.9 us -> 24.7 us
  other arithmetic: 4.36 us -> 0.73 us
    pallas_call x0 -> x4, Pallas kernels: none -> 57 us  [the longest x1 41 us: make_sums(): pl.pallas_call(sum_kernel, out_shape=jax.ShapeDtypeStruct((128, 16, 128),...]
    all_to_all x1 -> x0, blocking collectives: 50.3 us -> none  [local(): lax.all_to_all(buffer, ('tm', 'det'), split_axis=0, concat_axis=0, tiled=...]
    dot_general x6 -> x0, matrix products: 48.9 us -> none  [the longest x1 38.6 us: local(): jnp.einsum('gak,kcf->gcaf', precision_rows, sample_rows, preferred_elemen...]
    reshape x6 -> x1, local copies, waits for them, and re-layouts: 40.7 us -> 0.01 us  [local(): right = right_weight.reshape(128, 8, 4).transpose(2, 1, 0).reshape(32, 128)]
    convert_element_type x3 -> x0, local copies, waits for them, and re-layouts: 20.2 us -> none  [the longest x1 12 us: local(): frame_cube = jnp.einsum('gak,kcf->gcaf', precision_rows, sample_rows, pre...]
    unnamed x20 -> x12, local copies, waits for them, and re-layouts: 18.5 us -> 4.55 us
    all_to_all x1 -> x2, waiting for transfers between devices: 24.6 us -> 13.7 us  [the longest x1 13.7 us: local(): lax.all_to_all(sums, ('tm', 'det'), split_axis=0, concat_axis=0, tiled=True)]
    all_to_all x1 -> x2, starting transfers between devices: 8.24 us -> 19.1 us  [the longest x1 11 us: local(): lax.all_to_all(sums, ('tm', 'det'), split_axis=0, concat_axis=0, tiled=True)]
  transfers between devices with their start and end apart: 3 -> 4, of which waited for: 1 -> 1; matrix products, arithmetic and copies ran while one was open for 12% -> 1% of each run, Pallas kernels for 0% -> 14%
where the time goes in v1:
time: 103 us; the launch traced here: 102 us
  Pallas kernels  57 us (55%)
  starting transfers between devices  24.7 us (24%)
  waiting for transfers between devices  13.7 us (13%)
  local copies, waits for them, and re-layouts  5.27 us (5%)
    pallas_call x1, Pallas kernels, make_sums(): pl.pallas_call(sum_kernel, out_shape=jax.ShapeDtypeStruct((128, 16, 128),...  41 us
    all_to_all x1, waiting for transfers between devices, local(): lax.all_to_all(sums, ('tm', 'det'), split_axis=0, concat_axis=0, tiled=True)  13.7 us
    pallas_call x1, Pallas kernels, make_filtered(): pl.pallas_call(filter_kernel, out_shape=(jax.ShapeDtypeStruct((1024, 1024...  13 us
    all_to_all x1, starting transfers between devices, local(): lax.all_to_all(sums, ('tm', 'det'), split_axis=0, concat_axis=0, tiled=True)  11 us
    all_to_all x1, starting transfers between devices, local(): lists = lax.all_to_all(own, 'det', split_axis=0, concat_axis=0, tiled=True)  8.04 us
    unnamed x12, local copies, waits for them, and re-layouts  4.55 us
    ppermute x1, starting transfers between devices, local(): low = lax.ppermute(time_stream[:, -128:], 'tm', forward)  4.36 us
  transfers between devices with their start and end apart: 4, of which 1 were waited for; matrix products, arithmetic and copies ran while one was open for 1% of the time, Pallas kernels for 14%

profile of v1, /device:TPU:1, one launch (start us, length us, event | category | flops | bytes accessed | tf_op | source)
XLA Modules:
  0.0 102.1 jit_solution(2845177404066149391)
XLA Ops:
  0.0 0.7 fusion
  0.7 4.4 %collective-permute-start = (bf16[32,128]{1,0:T(8,128)(2,1)S(1)}, bf16[32,128]{1,0:T(8,128)(2,1)S(1)}, u32[]{:S(2)}, u32[]{:S(2)}) collective-permute-start(bf16[32,128]{1,0:T(8,128)(2,1)S(1)} %get-tuple-element.10), channel_id=1, source_target_pairs={{0,32},{32,64},{64,96},{1,33},{33,65},{65,97},{2,34},{34,66},{66,9... | collective-permute-start | bytes 24584 | tf_op jit(solution)/shard_map/ppermute | solution.py:213
  5.1 1.3 %collective-permute-start.1 = (bf16[32,128]{1,0:T(8,128)(2,1)S(1)}, bf16[32,128]{1,0:T(8,128)(2,1)S(1)}, u32[]{:S(2)}, u32[]{:S(2)}) collective-permute-start(bf16[32,128]{1,0:T(8,128)(2,1)S(1)} %get-tuple-element.9), channel_id=1, source_target_pairs={{32,0},{64,32},{96,64},{33,1},{65,33},{97,65},{34,2},{66,34},{98,6... | collective-permute-start | bytes 24584 | tf_op jit(solution)/shard_map/ppermute | solution.py:214
  7.0 0.0 copy-start.1
  7.0 0.7 copy-done.1
  7.7 0.0 copy-start.2
  7.7 0.7 copy-done.2
  8.4 1.2 %make_list.1 = f32[32,8,128]{2,1,0:T(8,128)} custom-call(s32[1]{0:T(128)S(6)} %copy.13.count_ref, s32[8,128]{1,0:T(8,128)S(1)} %bitcast.23, s32[1,256]{1,0:T(1,128)S(1)} %bitcast.24), custom_call_target="tpu_custom_call" | custom-call | flops 4000000 | bytes 200000 | tf_op jit(solution)/shard_map/make_list/pallas_call | solution.py:150
  9.6 8.0 %all-to-all-start = ((f32[32,8,128]{2,1,0:T(8,128)}), f32[32,8,128]{2,1,0:T(8,128)S(1)}, u32[]{:S(2)}, u32[]{:S(2)}) async-start(f32[32,8,128]{2,1,0:T(8,128)} %make_list.1), calls=%async_computation | async-start | bytes 262144 | tf_op jit(solution)/shard_map/all_to_all | solution.py:216
  17.7 0.7 pad_convert_fusion.taps_ref
  18.4 0.0 collective-permute-done
  18.4 0.0 collective-permute-done.1
  18.4 0.0 copy-start.3
  18.4 1.6 %copy-done.3 = bf16[32,32768]{1,0:T(8,128)(2,1)S(1)} copy-done((bf16[32,32768]{1,0:T(8,128)(2,1)S(1)}, bf16[32,32768]{1,0:T(8,128)(2,1)}, u32[]{:S(2)}) %copy-start.3) | copy-done | bytes 2097176
  20.0 0.0 copy-start.4
  20.0 1.6 %copy-done.4 = bf16[1024,1024]{1,0:T(8,128)(2,1)S(1)} copy-done((bf16[1024,1024]{1,0:T(8,128)(2,1)S(1)}, bf16[1024,1024]{1,0:T(8,128)(2,1)}, u32[]{:S(2)}) %copy-start.4) | copy-done | bytes 2097176
  21.6 13.0 %make_filtered.1 = (bf16[1024,1024]{1,0:T(8,128)(2,1)S(1)}, bf16[1024,256]{1,0:T(8,128)(2,1)S(1)}) custom-call(bf16[4,256,8,128]{3,2,1,0:T(8,128)(2,1)S(1)} %bitcast.25, bf16[4,8,128]{2,1,0:T(8,128)(2,1)S(1)} %bitcast.26, bf16[4,8,128]{2,1,0:T(8,128)(2,1)S(1)} %bitcast.27, f32[32,256]{1,0:T(8,128)S(1)} %pad_convert_fusion.taps_ref, ...), custom_call_target="tpu_custom_call" | custom-call | flops 5000000000 | bytes 7000000 | tf_op jit(solution)/shard_map/make_filtered/pallas_call | solution.py:162
  34.6 0.0 all-to-all-done
  34.6 0.0 copy-start.5
  34.6 0.0 copy-start
  34.6 41.0 %make_sums.1 = bf16[128,16,128]{2,1,0:T(8,128)(2,1)} custom-call(f32[256,128]{1,0:T(8,128)S(1)} %bitcast.20, bf16[1024,1024]{1,0:T(8,128)(2,1)S(1)} %get-tuple-element.7.b_ref, bf16[1024,256]{1,0:T(8,128)(2,1)S(1)} %get-tuple-element.8.rep_ref), custom_call_target="tpu_custom_call" | custom-call | flops 22000001024 | bytes 3000000 | tf_op jit(solution)/shard_map/make_sums/pallas_call | solution.py:175
  75.6 11.0 %all-to-all-start.1 = ((bf16[128,16,128]{2,1,0:T(8,128)(2,1)}), bf16[128,16,128]{2,1,0:T(8,128)(2,1)S(1)}, u32[]{:S(2)}, u32[]{:S(2)}) async-start(bf16[128,16,128]{2,1,0:T(8,128)(2,1)} %make_sums.1), calls=%async_computation.1 | async-start | bytes 1048576 | tf_op jit(solution)/shard_map/all_to_all | solution.py:222
  86.6 0.0 copy-done.5
  86.6 13.7 %all-to-all-done.1.in_ref = bf16[128,16,128]{2,1,0:T(8,128)(2,1)S(1)} async-done(((bf16[128,16,128]{2,1,0:T(8,128)(2,1)}), bf16[128,16,128]{2,1,0:T(8,128)(2,1)S(1)}, u32[]{:S(2)}, u32[]{:S(2)}) %all-to-all-start.1) | async-done | bytes 524320 | tf_op jit(solution)/shard_map/all_to_all | solution.py:222
  100.3 0.0 copy-done
  100.3 1.8 %make_tiles.1 = f32[256,128]{1,0:T(8,128)} custom-call(bf16[128,16,128]{2,1,0:T(8,128)(2,1)S(1)} %all-to-all-done.1.in_ref, f32[32,128]{1,0:T(8,128)S(1)} %bitcast.22, f32[32,128]{1,0:T(8,128)S(1)} %bitcast.21), custom_call_target="tpu_custom_call" | custom-call | flops 40000000 | bytes 700000 | tf_op jit(solution)/shard_map/make_tiles/pallas_call | solution.py:194
  (1 shorter events, 0.0 us)
Async XLA Ops:
  0.7 17.7 %collective-permute-start = (bf16[32,128]{1,0:T(8,128)(2,1)S(1)}, bf16[32,128]{1,0:T(8,128)(2,1)S(1)}, u32[]{:S(2)}, u32[]{:S(2)}) collective-permute-start(bf16[32,128]{1,0:T(8,128)(2,1)S(1)} %get-tuple-element.10), channel_id=1, source_target_pairs={{0,32},{32,64},{64,96},{1,33},{33,65},{65,97},{2,34},{34,66},{66,9... | collective-permute-start | bytes 24584 | tf_op jit(solution)/shard_map/ppermute | solution.py:213
  5.1 13.3 %collective-permute-start.1 = (bf16[32,128]{1,0:T(8,128)(2,1)S(1)}, bf16[32,128]{1,0:T(8,128)(2,1)S(1)}, u32[]{:S(2)}, u32[]{:S(2)}) collective-permute-start(bf16[32,128]{1,0:T(8,128)(2,1)S(1)} %get-tuple-element.9), channel_id=1, source_target_pairs={{32,0},{64,32},{96,64},{33,1},{65,33},{97,65},{34,2},{66,34},{98,6... | collective-permute-start | bytes 24584 | tf_op jit(solution)/shard_map/ppermute | solution.py:214
  7.0 0.7 copy-start.1
  7.7 0.7 copy-start.2
  9.6 25.0 %all-to-all-start = ((f32[32,8,128]{2,1,0:T(8,128)}), f32[32,8,128]{2,1,0:T(8,128)S(1)}, u32[]{:S(2)}, u32[]{:S(2)}) async-start(f32[32,8,128]{2,1,0:T(8,128)} %make_list.1), calls=%async_computation | async-start | bytes 262144 | tf_op jit(solution)/shard_map/all_to_all | solution.py:216
  18.4 1.6 %copy-start.3 = (bf16[32,32768]{1,0:T(8,128)(2,1)S(1)}, bf16[32,32768]{1,0:T(8,128)(2,1)}, u32[]{:S(2)}) copy-start(bf16[32,32768]{1,0:T(8,128)(2,1)} %param.8) | copy-start | bytes 6291460
  20.0 1.6 %copy-start.4 = (bf16[1024,1024]{1,0:T(8,128)(2,1)S(1)}, bf16[1024,1024]{1,0:T(8,128)(2,1)}, u32[]{:S(2)}) copy-start(bf16[1024,1024]{1,0:T(8,128)(2,1)} %precision_ref.1) | copy-start | bytes 6291460
  34.6 52.0 %copy-start.5 = (f32[128,32]{0,1:T(8,128)S(1)}, f32[128,32]{0,1:T(8,128)}, u32[]{:S(2)}) copy-start(f32[128,32]{0,1:T(8,128)} %param.12) | copy-start | bytes 49156
  34.6 65.7 %copy-start = (f32[128,32]{0,1:T(8,128)S(1)}, f32[128,32]{0,1:T(8,128)}, u32[]{:S(2)}) copy-start(f32[128,32]{0,1:T(8,128)} %param.11) | copy-start | bytes 49156
  75.6 24.7 %all-to-all-start.1 = ((bf16[128,16,128]{2,1,0:T(8,128)(2,1)}), bf16[128,16,128]{2,1,0:T(8,128)(2,1)S(1)}, u32[]{:S(2)}, u32[]{:S(2)}) async-start(bf16[128,16,128]{2,1,0:T(8,128)(2,1)} %make_sums.1), calls=%async_computation.1 | async-start | bytes 1048576 | tf_op jit(solution)/shard_map/all_to_all | solution.py:222

commit v2 on v1

--- a/solution.py
+++ b/solution.py
@@ -10,6 +10,7 @@
 F32 = jnp.float32
 BF16 = jnp.bfloat16
 ANY_NT = (((1,), (1,)), ((), ()))
+GROUPS = 8
 TN = (((0,), (0,)), ((), ()))
 
 
@@ -21,7 +22,18 @@
     return pltpu.CompilerParams(vmem_limit_bytes=mib << 20)
 
 
-def list_kernel(count_ref, tile_ref, owner_ref, out_ref):
+def prepare_kernel(count_hbm, tile_hbm, owner_hbm, x_hbm, out_ref, first_ref, last_ref, count_ref, tile_ref, owner_ref, sems):
+    copies = [
+        pltpu.make_async_copy(count_hbm, count_ref, sems.at[0]),
+        pltpu.make_async_copy(tile_hbm, tile_ref, sems.at[1]),
+        pltpu.make_async_copy(owner_hbm, owner_ref, sems.at[2]),
+        pltpu.make_async_copy(x_hbm.at[:, 0], first_ref, sems.at[3]),
+        pltpu.make_async_copy(x_hbm.at[:, 255], last_ref, sems.at[4]),
+    ]
+    for copy in copies:
+        copy.start()
+    for copy in copies:
+        copy.wait()
     owner = owner_ref[...]
     row, col = iota((256, 256), 0), iota((256, 256), 1)
     owner_col = jnp.sum(jnp.where(row == col, owner, 0), axis=1, keepdims=True)
@@ -60,14 +72,26 @@
     return arrays
 
 
-def filter_kernel(x_ref, low_ref, high_ref, taps_ref, precision_ref, b_ref, rep_ref, rows_ref, y_ref):
-    me = lax.axis_index("det")
-    chosen = jnp.where(iota((1024, 256), 0) - me * 32 == iota((1024, 256), 1) // 8, 1.0, 0.0).astype(BF16)
-    rep_ref[...] = jnp.dot(precision_ref[...], chosen, preferred_element_type=F32).astype(BF16)
+def filter_kernel(
+    x_hbm, low_ref, high_ref, taps_hbm, precision_hbm, b_ref, rep_ref,
+    x_ref, narrow_ref, taps_ref, precision_ref, rows_ref, y_ref, sems,
+):
+    taps_copy = pltpu.make_async_copy(taps_hbm, narrow_ref, sems.at[0])
+    taps_copy.start()
+    x_copies = [pltpu.make_async_copy(x_hbm.at[i], x_ref.at[i], sems.at[2 + i]) for i in range(4)]
+    for copy in x_copies:
+        copy.start()
+    precision_copy = pltpu.make_async_copy(precision_hbm, precision_ref, sems.at[1])
+    precision_copy.start()
+    taps_copy.wait()
+    taps_ref[:, :128] = narrow_ref[:, :128].astype(F32)
+    last = jnp.broadcast_to(narrow_ref[:, 128:129].astype(F32), (32, 128))
+    taps_ref[:, 128:] = jnp.where(iota((32, 128), 1) == 0, last, 0.0)
     first_half = iota((256, 128), 1) < 64
     for half in range(2):
         for g in range(2):
             dg = half * 2 + g
+            x_copies[dg].wait()
             rows_ref[0:8, :] = low_ref[dg].astype(F32)
             rows_ref[8 + 2048 : 16 + 2048, :] = high_ref[dg].astype(F32)
             rows_ref[8 : 8 + 2048, :] = x_ref[dg].astype(F32).reshape(2048, 128)
@@ -81,39 +105,48 @@
                 y_ref[g * 8 + d] = lax.dot_general(window, matrix, ANY_NT, preferred_element_type=F32)
 
         def chunk(i, carry):
-            at = pl.multiple_of(i * 16, 16)
-            out = butterfly([y_ref[e, pl.ds(at, 16), :] for e in range(16)], 8)
+            at = pl.multiple_of(i * 128, 128)
+            out = butterfly([y_ref[e, pl.ds(at, 128), :] for e in range(16)], 8)
             for q in range(16):
                 lanes = (q % 4) * 256 + half * 128
-                b_ref[pl.ds(pl.multiple_of((q // 4) * 256 + at, 16), 16), lanes : lanes + 128] = out[q].astype(BF16)
+                b_ref[pl.ds(pl.multiple_of((q // 4) * 256 + at, 128), 128), lanes : lanes + 128] = out[q].astype(BF16)
             return carry
 
-        lax.fori_loop(0, 16, chunk, 0)
+        lax.fori_loop(0, 2, chunk, 0)
+    me = lax.axis_index("det")
+    chosen = jnp.where(iota((1024, 256), 0) - me * 32 == iota((1024, 256), 1) // 8, 1.0, 0.0).astype(BF16)
+    precision_copy.wait()
+    rep_ref[...] = jnp.dot(precision_ref[...], chosen, preferred_element_type=F32).astype(BF16)
 
 
 def sum_kernel(list_ref, b_ref, rep_ref, out_ref, lists_ref, hot_ref, w_ref, acc_ref, rows_ref):
     lists_ref[...] = list_ref[...].T
-    number = iota((256, 256), 0).astype(F32)
+    number = iota((256, 256), 0).astype(F32).astype(BF16)
+    one, zero = jnp.ones((), BF16), jnp.zeros((), BF16)
     acc_ref[...] = jnp.zeros_like(acc_ref)
 
     def group(i, carry):
-        for g in range(4):
+        for g in range(GROUPS):
             for c in range(4):
-                names = lists_ref[pl.ds(i * 16 + g * 4 + c, 1), :]
-                hot_ref[g * 256 : (g + 1) * 256, c * 256 : (c + 1) * 256] = jnp.where(number == names, 1.0, 0.0).astype(BF16)
-            rep = rep_ref[pl.ds(pl.multiple_of(i * 128 + g * 32, 32), 32), :]
+                names = lists_ref[pl.ds(i * (4 * GROUPS) + g * 4 + c, 1), :].astype(BF16)
+                hot = jnp.where(number == jnp.broadcast_to(names, (256, 256)), one, zero)
+                hot_ref[g * 256 : (g + 1) * 256, c * 256 : (c + 1) * 256] = hot
+            rep = rep_ref[pl.ds(pl.multiple_of(i * (32 * GROUPS) + g * 32, 32), 32), :]
             for f in range(8):
                 w_ref[f * 32 : (f + 1) * 32, g * 256 : (g + 1) * 256] = jnp.where(
                     iota((32, 256), 1) % 8 == f, rep.astype(F32), 0.0
                 ).astype(BF16)
-        for n in range(4):
-            cols = slice(n * 256, (n + 1) * 256)
-            s = jnp.dot(hot_ref[...], b_ref[:, cols], preferred_element_type=F32).astype(BF16)
-            wide = jnp.concatenate([s[g * 256 : (g + 1) * 256] for g in range(4)], axis=1)
-            acc_ref[:, cols] += lax.dot_general(wide, w_ref[...], ANY_NT, preferred_element_type=F32)
+        for n in range(2):
+            s = jnp.dot(hot_ref[...], b_ref[:, n * 512 : (n + 1) * 512], preferred_element_type=F32).astype(BF16)
+            for m in range(2):
+                wide = jnp.concatenate(
+                    [s[g * 256 : (g + 1) * 256, m * 256 : (m + 1) * 256] for g in range(GROUPS)], axis=1
+                )
+                cols = slice(n * 512 + m * 256, n * 512 + m * 256 + 256)
+                acc_ref[:, cols] += lax.dot_general(wide, w_ref[...], ANY_NT, preferred_element_type=F32)
         return carry
 
-    lax.fori_loop(0, 8, group, 0)
+    lax.fori_loop(0, 32 // GROUPS, group, 0)
     for t in range(8):
         rows_ref[pl.ds(t, 256, stride=8), :] = acc_ref[:, t * 128 : (t + 1) * 128]
     out_ref[...] = rows_ref[...].astype(BF16).reshape(out_ref.shape)
@@ -146,26 +179,45 @@
     return [pl.BlockSpec(memory_space=pltpu.VMEM)] * n
 
 
-def make_list(frame_count, tiles, owner):
-    return pl.pallas_call(
-        list_kernel,
-        out_shape=jax.ShapeDtypeStruct((32, 8, 128), F32),
-        in_specs=[pl.BlockSpec(memory_space=pltpu.SMEM)] + vmem(2),
-        out_specs=vmem(1)[0],
-        compiler_params=params(16),
+def anywhere(n):
+    return [pl.BlockSpec(memory_space=pl.ANY)] * n
+
+
+def prepare(frame_count, tiles, owner, x):
+    block = jax.ShapeDtypeStruct((4, 8, 128), BF16)
+    return pl.pallas_call(
+        prepare_kernel,
+        out_shape=(jax.ShapeDtypeStruct((32, 8, 128), F32), block, block),
+        in_specs=anywhere(4),
+        out_specs=tuple(vmem(3)),
+        scratch_shapes=[
+            pltpu.SMEM((1,), jnp.int32),
+            pltpu.VMEM((8, 128), jnp.int32),
+            pltpu.VMEM((1, 256), jnp.int32),
+            pltpu.SemaphoreType.DMA((5,)),
+        ],
+        compiler_params=params(60),
         cost_estimate=pl.CostEstimate(flops=4_000_000, bytes_accessed=200_000, transcendentals=0),
-        name="make_list",
-    )(frame_count, tiles, owner)
+        name="prepare",
+    )(frame_count, tiles, owner, x)
 
 
 def make_filtered(x, low, high, taps, precision):
     return pl.pallas_call(
         filter_kernel,
         out_shape=(jax.ShapeDtypeStruct((1024, 1024), BF16), jax.ShapeDtypeStruct((1024, 256), BF16)),
-        in_specs=vmem(5),
+        in_specs=anywhere(1) + vmem(2) + anywhere(2),
         out_specs=tuple(vmem(2)),
-        scratch_shapes=[pltpu.VMEM((2064, 128), F32), pltpu.VMEM((16, 256, 128), F32)],
-        compiler_params=params(40),
+        scratch_shapes=[
+            pltpu.VMEM((4, 256, 8, 128), BF16),
+            pltpu.VMEM((32, 129), BF16),
+            pltpu.VMEM((32, 256), F32),
+            pltpu.VMEM((1024, 1024), BF16),
+            pltpu.VMEM((2064, 128), F32),
+            pltpu.VMEM((16, 256, 128), F32),
+            pltpu.SemaphoreType.DMA((6,)),
+        ],
+        compiler_params=params(51),
         cost_estimate=pl.CostEstimate(flops=5_000_000_000, bytes_accessed=7_000_000, transcendentals=0),
         name="make_filtered",
     )(x, low, high, taps, precision)
@@ -179,12 +231,12 @@
         out_specs=vmem(1)[0],
         scratch_shapes=[
             pltpu.VMEM((128, 256), F32),
-            pltpu.VMEM((1024, 1024), BF16),
-            pltpu.VMEM((256, 1024), BF16),
+            pltpu.VMEM((GROUPS * 256, 1024), BF16),
+            pltpu.VMEM((256, GROUPS * 256), BF16),
             pltpu.VMEM((256, 1024), F32),
             pltpu.VMEM((2048, 128), F32),
         ],
-        compiler_params=params(40),
+        compiler_params=params(44),
         cost_estimate=pl.CostEstimate(flops=22_000_000_000, bytes_accessed=3_000_000, transcendentals=0),
         name="make_sums",
     )(lists, filtered, rep)
@@ -210,14 +262,12 @@
     count = lax.axis_size("tm")
     forward = [(i, i + 1) for i in range(count - 1)]
     backward = [(j, i) for i, j in forward]
-    low = lax.ppermute(time_stream[:, -128:], "tm", forward)
-    high = lax.ppermute(time_stream[:, :128], "tm", backward)
-    own = make_list(frame_count, frame_tile.reshape(8, 128), tile_owner.reshape(1, 256))
+    x = split_rows(time_stream)
+    own, first, last = prepare(frame_count, frame_tile.reshape(8, 128), tile_owner.reshape(1, 256), x)
+    low = lax.ppermute(last, "tm", forward)
+    high = lax.ppermute(first, "tm", backward)
     lists = lax.all_to_all(own, "det", split_axis=0, concat_axis=0, tiled=True)
-    taps = jnp.pad(filter_taps.astype(F32), ((0, 0), (0, 256 - filter_taps.shape[1])))
-    filtered, rep = make_filtered(
-        split_rows(time_stream), low.reshape(4, 8, 128), high.reshape(4, 8, 128), taps, det_precision
-    )
+    filtered, rep = make_filtered(x, low, high, filter_taps, det_precision)
     sums = make_sums(lists.reshape(256, 128), filtered, rep)
     received = lax.all_to_all(sums, ("tm", "det"), split_axis=0, concat_axis=0, tiled=True)
     right = right_weight.reshape(128, 8, 4).transpose(2, 1, 0).reshape(32, 128)

time: 103 us -> 74.7 us (0.73)
  Pallas kernels: 57 us -> 35.1 us
  local copies, waits for them, and re-layouts: 5.27 us -> 0.02 us
    pallas_call x1, Pallas kernels: 41 us -> 23.7 us  [make_sums(): pl.pallas_call(sum_kernel, out_shape=jax.ShapeDtypeStruct((128, 16, 128),...]
    pallas_call x1, Pallas kernels: 13 us -> 7.6 us  [make_filtered(): pl.pallas_call(filter_kernel, out_shape=(jax.ShapeDtypeStruct((1024, 1024...]
    unnamed x12 -> x6, local copies, waits for them, and re-layouts: 4.55 us -> 0.02 us
  transfers between devices with their start and end apart: 4 -> 4, of which waited for: 1 -> 1; matrix products, arithmetic and copies ran while one was open for 1% -> 0% of each run, Pallas kernels for 14% -> 10%
where the time goes in v2:
time: 74.7 us; the launch traced here: 74.3 us
  Pallas kernels  35.1 us (47%)
  starting transfers between devices  24.7 us (33%)
  waiting for transfers between devices  13.7 us (18%)
  between operations  0.77 us (1%)
    pallas_call x1, Pallas kernels, make_sums(): pl.pallas_call(sum_kernel, out_shape=jax.ShapeDtypeStruct((128, 16, 128),...  23.7 us
    all_to_all x1, waiting for transfers between devices, local(): lax.all_to_all(sums, ('tm', 'det'), split_axis=0, concat_axis=0, tiled=True)  13.7 us
    all_to_all x1, starting transfers between devices, local(): lax.all_to_all(sums, ('tm', 'det'), split_axis=0, concat_axis=0, tiled=True)  11 us
    all_to_all x1, starting transfers between devices, local(): lists = lax.all_to_all(own, 'det', split_axis=0, concat_axis=0, tiled=True)  8.05 us
    pallas_call x1, Pallas kernels, make_filtered(): pl.pallas_call(filter_kernel, out_shape=(jax.ShapeDtypeStruct((1024, 1024...  7.6 us
    ppermute x1, starting transfers between devices, local(): low = lax.ppermute(last, 'tm', forward)  4.37 us
    pallas_call x1, Pallas kernels, prepare(): pl.pallas_call(prepare_kernel, out_shape=(jax.ShapeDtypeStruct((32, 8, 12...  2.02 us
    pallas_call x1, Pallas kernels, make_tiles(): pl.pallas_call(tile_kernel, out_shape=jax.ShapeDtypeStruct((256, 128), F3...  1.77 us
  transfers between devices with their start and end apart: 4, of which 1 were waited for; matrix products, arithmetic and copies ran while one was open for 0% of the time, Pallas kernels for 10%

profile of v2, /device:TPU:1, one launch (start us, length us, event | category | flops | bytes accessed | tf_op | source)
XLA Modules:
  0.0 74.3 jit_solution(14932402426638058458)
XLA Ops:
  0.0 0.0 copy-start.1
  0.7 2.0 %prepare.1 = (f32[32,8,128]{2,1,0:T(8,128)}, bf16[4,8,128]{2,1,0:T(8,128)(2,1)}, bf16[4,8,128]{2,1,0:T(8,128)(2,1)}) custom-call(s32[1]{0:T(128)S(6)} %copy.13.count_hbm, s32[8,128]{1,0:T(8,128)} %bitcast.24, s32[1,256]{1,0:T(1,128)} %bitcast.25, bf16[4,256,8,128]{3,2,1,0:T(8,128)(2,1)} %bitcast.21), custom_call_target="tpu_custom_call" | custom-call | flops 4000000 | bytes 200000 | tf_op jit(solution)/shard_map/prepare/pallas_call | solution.py:188
  2.7 4.4 %collective-permute-start = (bf16[4,8,128]{2,1,0:T(8,128)(2,1)}, bf16[4,8,128]{2,1,0:T(8,128)(2,1)S(1)}, u32[]{:S(2)}, u32[]{:S(2)}) collective-permute-start(bf16[4,8,128]{2,1,0:T(8,128)(2,1)} %get-tuple-element.11), channel_id=1, source_target_pairs={{0,32},{32,64},{64,96},{1,33},{33,65},{65,97},{2,34},{34,66},{66,9... | collective-permute-start | bytes 24584 | tf_op jit(solution)/shard_map/ppermute | solution.py:267
  7.1 1.3 %collective-permute-start.1 = (bf16[4,8,128]{2,1,0:T(8,128)(2,1)}, bf16[4,8,128]{2,1,0:T(8,128)(2,1)S(1)}, u32[]{:S(2)}, u32[]{:S(2)}) collective-permute-start(bf16[4,8,128]{2,1,0:T(8,128)(2,1)} %get-tuple-element.12), channel_id=1, source_target_pairs={{32,0},{64,32},{96,64},{33,1},{65,33},{97,65},{34,2},{66,34},{98,6... | collective-permute-start | bytes 24584 | tf_op jit(solution)/shard_map/ppermute | solution.py:268
  8.4 8.1 %all-to-all-start = ((f32[32,8,128]{2,1,0:T(8,128)}), f32[32,8,128]{2,1,0:T(8,128)S(1)}, u32[]{:S(2)}, u32[]{:S(2)}) async-start(f32[32,8,128]{2,1,0:T(8,128)} %get-tuple-element.10), calls=%async_computation | async-start | bytes 262144 | tf_op jit(solution)/shard_map/all_to_all | solution.py:269
  16.4 0.0 collective-permute-done.low_ref
  16.4 0.0 collective-permute-done.1.high_ref
  16.5 0.0 copy-done.1
  16.5 7.6 %make_filtered.1 = (bf16[1024,1024]{1,0:T(8,128)(2,1)S(1)}, bf16[1024,256]{1,0:T(8,128)(2,1)S(1)}) custom-call(bf16[4,256,8,128]{3,2,1,0:T(8,128)(2,1)} %bitcast.22, bf16[4,8,128]{2,1,0:T(8,128)(2,1)S(1)} %collective-permute-done.low_ref, bf16[4,8,128]{2,1,0:T(8,128)(2,1)S(1)} %collective-permute-done.1.high_ref, bf16[32,129]{1,0:T(8,128)(2,1)S(1)} %copy-done.1, ...), custom_call_target="tpu_custom_call" | custom-call | flops 5000000000 | bytes 7000000 | tf_op jit(solution)/shard_map/make_filtered/pallas_call | solution.py:206
  24.1 0.0 all-to-all-done
  24.1 0.0 copy-start.2
  24.1 0.0 copy-start
  24.1 23.7 %make_sums.1 = bf16[128,16,128]{2,1,0:T(8,128)(2,1)} custom-call(f32[256,128]{1,0:T(8,128)S(1)} %bitcast.18, bf16[1024,1024]{1,0:T(8,128)(2,1)S(1)} %get-tuple-element.13.b_ref, bf16[1024,256]{1,0:T(8,128)(2,1)S(1)} %get-tuple-element.14.rep_ref), custom_call_target="tpu_custom_call" | custom-call | flops 22000001024 | bytes 3000000 | tf_op jit(solution)/shard_map/make_sums/pallas_call | solution.py:227
  47.8 11.0 %all-to-all-start.1 = ((bf16[128,16,128]{2,1,0:T(8,128)(2,1)}), bf16[128,16,128]{2,1,0:T(8,128)(2,1)S(1)}, u32[]{:S(2)}, u32[]{:S(2)}) async-start(bf16[128,16,128]{2,1,0:T(8,128)(2,1)} %make_sums.1), calls=%async_computation.1 | async-start | bytes 1048576 | tf_op jit(solution)/shard_map/all_to_all | solution.py:272
  58.8 0.0 copy-done.2
  58.9 13.7 %all-to-all-done.1.in_ref = bf16[128,16,128]{2,1,0:T(8,128)(2,1)S(1)} async-done(((bf16[128,16,128]{2,1,0:T(8,128)(2,1)}), bf16[128,16,128]{2,1,0:T(8,128)(2,1)S(1)}, u32[]{:S(2)}, u32[]{:S(2)}) %all-to-all-start.1) | async-done | bytes 524320 | tf_op jit(solution)/shard_map/all_to_all | solution.py:272
  72.6 0.0 copy-done
  72.6 1.8 %make_tiles.1 = f32[256,128]{1,0:T(8,128)} custom-call(bf16[128,16,128]{2,1,0:T(8,128)(2,1)S(1)} %all-to-all-done.1.in_ref, f32[32,128]{1,0:T(8,128)S(1)} %bitcast.20, f32[32,128]{1,0:T(8,128)S(1)} %bitcast.19), custom_call_target="tpu_custom_call" | custom-call | flops 40000000 | bytes 700000 | tf_op jit(solution)/shard_map/make_tiles/pallas_call | solution.py:246
  (1 shorter events, 0.0 us)
Async XLA Ops:
  0.0 16.5 %copy-start.1 = (bf16[32,129]{1,0:T(8,128)(2,1)S(1)}, bf16[32,129]{1,0:T(8,128)(2,1)}, u32[]{:S(2)}) copy-start(bf16[32,129]{1,0:T(8,128)(2,1)} %taps_hbm.1) | copy-start | bytes 24772
  2.7 13.7 %collective-permute-start = (bf16[4,8,128]{2,1,0:T(8,128)(2,1)}, bf16[4,8,128]{2,1,0:T(8,128)(2,1)S(1)}, u32[]{:S(2)}, u32[]{:S(2)}) collective-permute-start(bf16[4,8,128]{2,1,0:T(8,128)(2,1)} %get-tuple-element.11), channel_id=1, source_target_pairs={{0,32},{32,64},{64,96},{1,33},{33,65},{65,97},{2,34},{34,66},{66,9... | collective-permute-start | bytes 24584 | tf_op jit(solution)/shard_map/ppermute | solution.py:267
  7.1 9.4 %collective-permute-start.1 = (bf16[4,8,128]{2,1,0:T(8,128)(2,1)}, bf16[4,8,128]{2,1,0:T(8,128)(2,1)S(1)}, u32[]{:S(2)}, u32[]{:S(2)}) collective-permute-start(bf16[4,8,128]{2,1,0:T(8,128)(2,1)} %get-tuple-element.12), channel_id=1, source_target_pairs={{32,0},{64,32},{96,64},{33,1},{65,33},{97,65},{34,2},{66,34},{98,6... | collective-permute-start | bytes 24584 | tf_op jit(solution)/shard_map/ppermute | solution.py:268
  8.4 15.7 %all-to-all-start = ((f32[32,8,128]{2,1,0:T(8,128)}), f32[32,8,128]{2,1,0:T(8,128)S(1)}, u32[]{:S(2)}, u32[]{:S(2)}) async-start(f32[32,8,128]{2,1,0:T(8,128)} %get-tuple-element.10), calls=%async_computation | async-start | bytes 262144 | tf_op jit(solution)/shard_map/all_to_all | solution.py:269
  24.1 34.8 %copy-start.2 = (f32[128,32]{0,1:T(8,128)S(1)}, f32[128,32]{0,1:T(8,128)}, u32[]{:S(2)}) copy-start(f32[128,32]{0,1:T(8,128)} %param.12) | copy-start | bytes 49156
  24.1 48.5 %copy-start = (f32[128,32]{0,1:T(8,128)S(1)}, f32[128,32]{0,1:T(8,128)}, u32[]{:S(2)}) copy-start(f32[128,32]{0,1:T(8,128)} %param.11) | copy-start | bytes 49156
  47.8 24.8 %all-to-all-start.1 = ((bf16[128,16,128]{2,1,0:T(8,128)(2,1)}), bf16[128,16,128]{2,1,0:T(8,128)(2,1)S(1)}, u32[]{:S(2)}, u32[]{:S(2)}) async-start(bf16[128,16,128]{2,1,0:T(8,128)(2,1)} %make_sums.1), calls=%async_computation.1 | async-start | bytes 1048576 | tf_op jit(solution)/shard_map/all_to_all | solution.py:272

commit v3 on v2

--- a/solution.py
+++ b/solution.py
@@ -40,7 +40,7 @@
     rank = jnp.sum(jnp.where((owner_col == owner) & (col < row), 1, 0), axis=1, keepdims=True)
     dest_col = owner_col * 2 + rank
     number = iota((256, 128), 0)
-    count = count_ref[0]
+    count = count_ref[...]
     rows = []
     for r in range(8):
         tile = tile_ref[r : r + 1, :]
@@ -81,19 +81,24 @@
     x_copies = [pltpu.make_async_copy(x_hbm.at[i], x_ref.at[i], sems.at[2 + i]) for i in range(4)]
     for copy in x_copies:
         copy.start()
-    precision_copy = pltpu.make_async_copy(precision_hbm, precision_ref, sems.at[1])
+    me = lax.axis_index("det")
+    block = pl.multiple_of((me // 4) * 128, 128)
+    precision_copy = pltpu.make_async_copy(precision_hbm.at[:, pl.ds(block, 128)], precision_ref, sems.at[1])
     precision_copy.start()
     taps_copy.wait()
     taps_ref[:, :128] = narrow_ref[:, :128].astype(F32)
     last = jnp.broadcast_to(narrow_ref[:, 128:129].astype(F32), (32, 128))
     taps_ref[:, 128:] = jnp.where(iota((32, 128), 1) == 0, last, 0.0)
     first_half = iota((256, 128), 1) < 64
+    tm = lax.axis_index("tm")
+    has_low = jnp.where(tm > 0, 1.0, 0.0)
+    has_high = jnp.where(tm < lax.axis_size("tm") - 1, 1.0, 0.0)
     for half in range(2):
         for g in range(2):
             dg = half * 2 + g
             x_copies[dg].wait()
-            rows_ref[0:8, :] = low_ref[dg].astype(F32)
-            rows_ref[8 + 2048 : 16 + 2048, :] = high_ref[dg].astype(F32)
+            rows_ref[0:8, :] = low_ref[dg].astype(F32) * has_low
+            rows_ref[8 + 2048 : 16 + 2048, :] = high_ref[dg].astype(F32) * has_high
             rows_ref[8 : 8 + 2048, :] = x_ref[dg].astype(F32).reshape(2048, 128)
             for d in range(8):
                 before = rows_ref[pl.ds(d, 256, stride=8), :]
@@ -113,8 +118,7 @@
             return carry
 
         lax.fori_loop(0, 2, chunk, 0)
-    me = lax.axis_index("det")
-    chosen = jnp.where(iota((1024, 256), 0) - me * 32 == iota((1024, 256), 1) // 8, 1.0, 0.0).astype(BF16)
+    chosen = jnp.where(iota((128, 256), 0) - (me % 4) * 32 == iota((128, 256), 1) // 8, 1.0, 0.0).astype(BF16)
     precision_copy.wait()
     rep_ref[...] = jnp.dot(precision_ref[...], chosen, preferred_element_type=F32).astype(BF16)
 
@@ -191,7 +195,7 @@
         in_specs=anywhere(4),
         out_specs=tuple(vmem(3)),
         scratch_shapes=[
-            pltpu.SMEM((1,), jnp.int32),
+            pltpu.VMEM((1, 1), jnp.int32),
             pltpu.VMEM((8, 128), jnp.int32),
             pltpu.VMEM((1, 256), jnp.int32),
             pltpu.SemaphoreType.DMA((5,)),
@@ -212,7 +216,7 @@
             pltpu.VMEM((4, 256, 8, 128), BF16),
             pltpu.VMEM((32, 129), BF16),
             pltpu.VMEM((32, 256), F32),
-            pltpu.VMEM((1024, 1024), BF16),
+            pltpu.VMEM((1024, 128), BF16),
             pltpu.VMEM((2064, 128), F32),
             pltpu.VMEM((16, 256, 128), F32),
             pltpu.SemaphoreType.DMA((6,)),
@@ -260,10 +264,10 @@
 
 def local(time_stream, filter_taps, det_precision, left_weight, right_weight, frame_tile, tile_owner, frame_count):
     count = lax.axis_size("tm")
-    forward = [(i, i + 1) for i in range(count - 1)]
+    forward = [(i, (i + 1) % count) for i in range(count)]
     backward = [(j, i) for i, j in forward]
     x = split_rows(time_stream)
-    own, first, last = prepare(frame_count, frame_tile.reshape(8, 128), tile_owner.reshape(1, 256), x)
+    own, first, last = prepare(frame_count.reshape(1, 1), frame_tile.reshape(8, 128), tile_owner.reshape(1, 256), x)
     low = lax.ppermute(last, "tm", forward)
     high = lax.ppermute(first, "tm", backward)
     lists = lax.all_to_all(own, "det", split_axis=0, concat_axis=0, tiled=True)

time: 74.7 us -> 70.4 us (0.942)
  starting transfers between devices: 24.7 us -> 20.5 us
    all_to_all x1, starting transfers between devices: 11 us -> 7.73 us  [local(): lax.all_to_all(sums, ('tm', 'det'), split_axis=0, concat_axis=0, tiled=True)]
    ppermute x1, starting transfers between devices: 4.37 us -> 2.54 us  [local(): low = lax.ppermute(last, 'tm', forward)]
    ppermute x1, starting transfers between devices: 1.29 us -> 2.2 us  [local(): high = lax.ppermute(first, 'tm', backward)]
  transfers between devices with their start and end apart: 4 -> 4, of which waited for: 1 -> 2; matrix products, arithmetic and copies ran while one was open for 0% -> 0% of each run, Pallas kernels for 10% -> 10%
where the time goes in v3:
time: 70.4 us; the launch traced here: 70.1 us
  Pallas kernels  34.6 us (49%)
  starting transfers between devices  20.5 us (29%)
  waiting for transfers between devices  14.2 us (20%)
  between operations  0.74 us (1%)
    pallas_call x1, Pallas kernels, make_sums(): pl.pallas_call(sum_kernel, out_shape=jax.ShapeDtypeStruct((128, 16, 128),...  23.7 us
    all_to_all x1, waiting for transfers between devices, local(): lax.all_to_all(sums, ('tm', 'det'), split_axis=0, concat_axis=0, tiled=True)  13.7 us
    all_to_all x1, starting transfers between devices, local(): lists = lax.all_to_all(own, 'det', split_axis=0, concat_axis=0, tiled=True)  8.04 us
    all_to_all x1, starting transfers between devices, local(): lax.all_to_all(sums, ('tm', 'det'), split_axis=0, concat_axis=0, tiled=True)  7.73 us
    pallas_call x1, Pallas kernels, make_filtered(): pl.pallas_call(filter_kernel, out_shape=(jax.ShapeDtypeStruct((1024, 1024...  7.1 us
    ppermute x1, starting transfers between devices, local(): low = lax.ppermute(last, 'tm', forward)  2.54 us
    ppermute x1, starting transfers between devices, local(): high = lax.ppermute(first, 'tm', backward)  2.2 us
    pallas_call x1, Pallas kernels, prepare(): pl.pallas_call(prepare_kernel, out_shape=(jax.ShapeDtypeStruct((32, 8, 12...  2.05 us
  transfers between devices with their start and end apart: 4, of which 2 were waited for; matrix products, arithmetic and copies ran while one was open for 0% of the time, Pallas kernels for 10%

profile of v3, /device:TPU:1, one launch (start us, length us, event | category | flops | bytes accessed | tf_op | source)
XLA Modules:
  0.0 70.1 jit_solution(3958954295536103958)
XLA Ops:
  0.0 0.0 copy-start.1
  0.7 2.1 %prepare.1 = (f32[32,8,128]{2,1,0:T(8,128)}, bf16[4,8,128]{2,1,0:T(8,128)(2,1)}, bf16[4,8,128]{2,1,0:T(8,128)(2,1)}) custom-call(s32[1,1]{1,0:T(1,128)} %bitcast.19.count_hbm, s32[8,128]{1,0:T(8,128)} %bitcast.26, s32[1,256]{1,0:T(1,128)} %bitcast.27, bf16[4,256,8,128]{3,2,1,0:T(8,128)(2,1)} %bitcast.23), custom_call_target="tpu_custom_call" | custom-call | flops 4000000 | bytes 200000 | tf_op jit(solution)/shard_map/prepare/pallas_call | solution.py:192
  2.7 2.5 %collective-permute-start = (bf16[4,8,128]{2,1,0:T(8,128)(2,1)}, bf16[4,8,128]{2,1,0:T(8,128)(2,1)S(1)}, u32[]{:S(2)}, u32[]{:S(2)}) collective-permute-start(bf16[4,8,128]{2,1,0:T(8,128)(2,1)} %get-tuple-element.11), channel_id=1, source_target_pairs={{0,32},{32,64},{64,96},{96,0},{1,33},{33,65},{65,97},{97,1},{2,34}... | collective-permute-start | bytes 24584 | tf_op jit(solution)/shard_map/ppermute | solution.py:271
  5.3 2.2 %collective-permute-start.1 = (bf16[4,8,128]{2,1,0:T(8,128)(2,1)}, bf16[4,8,128]{2,1,0:T(8,128)(2,1)S(1)}, u32[]{:S(2)}, u32[]{:S(2)}) collective-permute-start(bf16[4,8,128]{2,1,0:T(8,128)(2,1)} %get-tuple-element.12), channel_id=1, source_target_pairs={{32,0},{64,32},{96,64},{0,96},{33,1},{65,33},{97,65},{1,97},{34,2}... | collective-permute-start | bytes 24584 | tf_op jit(solution)/shard_map/ppermute | solution.py:272
  7.5 8.0 %all-to-all-start = ((f32[32,8,128]{2,1,0:T(8,128)}), f32[32,8,128]{2,1,0:T(8,128)S(1)}, u32[]{:S(2)}, u32[]{:S(2)}) async-start(f32[32,8,128]{2,1,0:T(8,128)} %get-tuple-element.10), calls=%async_computation | async-start | bytes 262144 | tf_op jit(solution)/shard_map/all_to_all | solution.py:273
  15.5 0.0 collective-permute-done.low_ref
  15.5 0.0 collective-permute-done.1.high_ref
  15.5 0.0 copy-done.1
  15.5 7.1 %make_filtered.1 = (bf16[1024,1024]{1,0:T(8,128)(2,1)S(1)}, bf16[1024,256]{1,0:T(8,128)(2,1)S(1)}) custom-call(bf16[4,256,8,128]{3,2,1,0:T(8,128)(2,1)} %bitcast.24, bf16[4,8,128]{2,1,0:T(8,128)(2,1)S(1)} %collective-permute-done.low_ref, bf16[4,8,128]{2,1,0:T(8,128)(2,1)S(1)} %collective-permute-done.1.high_ref, bf16[32,129]{1,0:T(8,128)(2,1)S(1)} %copy-done.1, ...), custom_call_target="tpu_custom_call" | custom-call | flops 5000000000 | bytes 7000000 | tf_op jit(solution)/shard_map/make_filtered/pallas_call | solution.py:210
  22.6 0.5 all-to-all-done
  23.1 0.0 copy-start.2
  23.1 0.0 copy-start
  23.1 23.7 %make_sums.1 = bf16[128,16,128]{2,1,0:T(8,128)(2,1)} custom-call(f32[256,128]{1,0:T(8,128)S(1)} %bitcast.20, bf16[1024,1024]{1,0:T(8,128)(2,1)S(1)} %get-tuple-element.13.b_ref, bf16[1024,256]{1,0:T(8,128)(2,1)S(1)} %get-tuple-element.14.rep_ref), custom_call_target="tpu_custom_call" | custom-call | flops 22000001024 | bytes 3000000 | tf_op jit(solution)/shard_map/make_sums/pallas_call | solution.py:231
  46.8 7.7 %all-to-all-start.1 = ((bf16[128,16,128]{2,1,0:T(8,128)(2,1)}), bf16[128,16,128]{2,1,0:T(8,128)(2,1)S(1)}, u32[]{:S(2)}, u32[]{:S(2)}) async-start(bf16[128,16,128]{2,1,0:T(8,128)(2,1)} %make_sums.1), calls=%async_computation.1 | async-start | bytes 1048576 | tf_op jit(solution)/shard_map/all_to_all | solution.py:276
  54.6 0.0 copy-done.2
  54.6 13.7 %all-to-all-done.1.in_ref = bf16[128,16,128]{2,1,0:T(8,128)(2,1)S(1)} async-done(((bf16[128,16,128]{2,1,0:T(8,128)(2,1)}), bf16[128,16,128]{2,1,0:T(8,128)(2,1)S(1)}, u32[]{:S(2)}, u32[]{:S(2)}) %all-to-all-start.1) | async-done | bytes 524320 | tf_op jit(solution)/shard_map/all_to_all | solution.py:276
  68.3 0.0 copy-done
  68.3 1.8 %make_tiles.1 = f32[256,128]{1,0:T(8,128)} custom-call(bf16[128,16,128]{2,1,0:T(8,128)(2,1)S(1)} %all-to-all-done.1.in_ref, f32[32,128]{1,0:T(8,128)S(1)} %bitcast.22, f32[32,128]{1,0:T(8,128)S(1)} %bitcast.21), custom_call_target="tpu_custom_call" | custom-call | flops 40000000 | bytes 700000 | tf_op jit(solution)/shard_map/make_tiles/pallas_call | solution.py:250
  (1 shorter events, 0.0 us)
Async XLA Ops:
  0.0 15.5 %copy-start.1 = (bf16[32,129]{1,0:T(8,128)(2,1)S(1)}, bf16[32,129]{1,0:T(8,128)(2,1)}, u32[]{:S(2)}) copy-start(bf16[32,129]{1,0:T(8,128)(2,1)} %taps_hbm.1) | copy-start | bytes 24772
  2.7 12.8 %collective-permute-start = (bf16[4,8,128]{2,1,0:T(8,128)(2,1)}, bf16[4,8,128]{2,1,0:T(8,128)(2,1)S(1)}, u32[]{:S(2)}, u32[]{:S(2)}) collective-permute-start(bf16[4,8,128]{2,1,0:T(8,128)(2,1)} %get-tuple-element.11), channel_id=1, source_target_pairs={{0,32},{32,64},{64,96},{96,0},{1,33},{33,65},{65,97},{97,1},{2,34}... | collective-permute-start | bytes 24584 | tf_op jit(solution)/shard_map/ppermute | solution.py:271
  5.3 10.3 %collective-permute-start.1 = (bf16[4,8,128]{2,1,0:T(8,128)(2,1)}, bf16[4,8,128]{2,1,0:T(8,128)(2,1)S(1)}, u32[]{:S(2)}, u32[]{:S(2)}) collective-permute-start(bf16[4,8,128]{2,1,0:T(8,128)(2,1)} %get-tuple-element.12), channel_id=1, source_target_pairs={{32,0},{64,32},{96,64},{0,96},{33,1},{65,33},{97,65},{1,97},{34,2}... | collective-permute-start | bytes 24584 | tf_op jit(solution)/shard_map/ppermute | solution.py:272
  7.5 15.7 %all-to-all-start = ((f32[32,8,128]{2,1,0:T(8,128)}), f32[32,8,128]{2,1,0:T(8,128)S(1)}, u32[]{:S(2)}, u32[]{:S(2)}) async-start(f32[32,8,128]{2,1,0:T(8,128)} %get-tuple-element.10), calls=%async_computation | async-start | bytes 262144 | tf_op jit(solution)/shard_map/all_to_all | solution.py:273
  23.1 31.5 %copy-start.2 = (f32[128,32]{0,1:T(8,128)S(1)}, f32[128,32]{0,1:T(8,128)}, u32[]{:S(2)}) copy-start(f32[128,32]{0,1:T(8,128)} %param.12) | copy-start | bytes 49156
  23.1 45.2 %copy-start = (f32[128,32]{0,1:T(8,128)S(1)}, f32[128,32]{0,1:T(8,128)}, u32[]{:S(2)}) copy-start(f32[128,32]{0,1:T(8,128)} %param.11) | copy-start | bytes 49156
  46.8 21.5 %all-to-all-start.1 = ((bf16[128,16,128]{2,1,0:T(8,128)(2,1)}), bf16[128,16,128]{2,1,0:T(8,128)(2,1)S(1)}, u32[]{:S(2)}, u32[]{:S(2)}) async-start(bf16[128,16,128]{2,1,0:T(8,128)(2,1)} %make_sums.1), calls=%async_computation.1 | async-start | bytes 1048576 | tf_op jit(solution)/shard_map/all_to_all | solution.py:276

commit v4 on v3

--- a/solution.py
+++ b/solution.py
@@ -10,7 +10,7 @@
 F32 = jnp.float32
 BF16 = jnp.bfloat16
 ANY_NT = (((1,), (1,)), ((), ()))
-GROUPS = 8
+GROUPS = 4
 TN = (((0,), (0,)), ((), ()))
 
 
@@ -60,20 +60,21 @@
 
 def butterfly(arrays, chunk):
     lane = iota(arrays[0].shape, 1)
-    for bit in range(4):
-        step = 1 << bit
+    step = 1
+    while step < len(arrays):
         low = (lane // (chunk * step)) % 2 == 0
-        for i in range(16):
+        for i in range(len(arrays)):
             if i & step:
                 continue
             a, b = arrays[i], arrays[i + step]
             arrays[i] = jnp.where(low, a, pltpu.roll(b, chunk * step, 1))
             arrays[i + step] = jnp.where(low, pltpu.roll(a, 128 - chunk * step, 1), b)
+        step *= 2
     return arrays
 
 
 def filter_kernel(
-    x_hbm, low_ref, high_ref, taps_hbm, precision_hbm, b_ref, rep_ref,
+    x_hbm, low_ref, high_ref, taps_hbm, precision_hbm, own_ref, send_ref, rep_ref,
     x_ref, narrow_ref, taps_ref, precision_ref, rows_ref, y_ref, sems,
 ):
     taps_copy = pltpu.make_async_copy(taps_hbm, narrow_ref, sems.at[0])
@@ -81,8 +82,8 @@
     x_copies = [pltpu.make_async_copy(x_hbm.at[i], x_ref.at[i], sems.at[2 + i]) for i in range(4)]
     for copy in x_copies:
         copy.start()
-    me = lax.axis_index("det")
-    block = pl.multiple_of((me // 4) * 128, 128)
+    chip, core = lax.axis_index("chip"), lax.axis_index("core")
+    block = pl.multiple_of((chip // 2) * 128, 128)
     precision_copy = pltpu.make_async_copy(precision_hbm.at[:, pl.ds(block, 128)], precision_ref, sems.at[1])
     precision_copy.start()
     taps_copy.wait()
@@ -93,39 +94,43 @@
     tm = lax.axis_index("tm")
     has_low = jnp.where(tm > 0, 1.0, 0.0)
     has_high = jnp.where(tm < lax.axis_size("tm") - 1, 1.0, 0.0)
-    for half in range(2):
-        for g in range(2):
-            dg = half * 2 + g
-            x_copies[dg].wait()
-            rows_ref[0:8, :] = low_ref[dg].astype(F32) * has_low
-            rows_ref[8 + 2048 : 16 + 2048, :] = high_ref[dg].astype(F32) * has_high
-            rows_ref[8 : 8 + 2048, :] = x_ref[dg].astype(F32).reshape(2048, 128)
-            for d in range(8):
-                before = rows_ref[pl.ds(d, 256, stride=8), :]
-                here = rows_ref[pl.ds(8 + d, 256, stride=8), :]
-                after = rows_ref[pl.ds(16 + d, 256, stride=8), :]
-                window = jnp.concatenate([here, jnp.where(first_half, after, before)], axis=1).astype(BF16)
-                taps = jnp.broadcast_to(taps_ref[dg * 8 + d : dg * 8 + d + 1, :], (128, 256))
-                matrix = pltpu.roll(taps, 192, 1, stride=1, stride_axis=0).astype(BF16)
-                y_ref[g * 8 + d] = lax.dot_general(window, matrix, ANY_NT, preferred_element_type=F32)
-
-        def chunk(i, carry):
-            at = pl.multiple_of(i * 128, 128)
-            out = butterfly([y_ref[e, pl.ds(at, 128), :] for e in range(16)], 8)
-            for q in range(16):
-                lanes = (q % 4) * 256 + half * 128
-                b_ref[pl.ds(pl.multiple_of((q // 4) * 256 + at, 128), 128), lanes : lanes + 128] = out[q].astype(BF16)
+    for dg in range(4):
+        x_copies[dg].wait()
+        rows_ref[0:8, :] = low_ref[dg].astype(F32) * has_low
+        rows_ref[8 + 2048 : 16 + 2048, :] = high_ref[dg].astype(F32) * has_high
+        rows_ref[8 : 8 + 2048, :] = x_ref[dg].astype(F32).reshape(2048, 128)
+        for d in range(8):
+            before = rows_ref[pl.ds(d, 256, stride=8), :]
+            here = rows_ref[pl.ds(8 + d, 256, stride=8), :]
+            after = rows_ref[pl.ds(16 + d, 256, stride=8), :]
+            window = jnp.concatenate([here, jnp.where(first_half, after, before)], axis=1).astype(BF16)
+            taps = jnp.broadcast_to(taps_ref[dg * 8 + d : dg * 8 + d + 1, :], (128, 256))
+            matrix = pltpu.roll(taps, 192, 1, stride=1, stride_axis=0).astype(BF16)
+            y = lax.dot_general(window, matrix, ANY_NT, preferred_element_type=F32)
+            y_ref[dg * 8 + d] = y.reshape(16, 2, 8, 128)
+    for parity, to_ref in ((1 - core, send_ref), (core, own_ref)):
+
+        def chunk(i, carry, parity=parity, to_ref=to_ref):
+            out = butterfly([y_ref[e, pl.ds(i * 8, 8), parity].reshape(64, 128) for e in range(32)], 4)
+            for q in range(32):
+                at = pl.multiple_of((q // 8) * 128 + i * 64, 64)
+                to_ref[pl.ds(at, 64), (q % 8) * 128 : (q % 8 + 1) * 128] = out[q].astype(BF16)
             return carry
 
         lax.fori_loop(0, 2, chunk, 0)
-    chosen = jnp.where(iota((128, 256), 0) - (me % 4) * 32 == iota((128, 256), 1) // 8, 1.0, 0.0).astype(BF16)
+    place = iota((128, 256), 1)
+    wanted = (chip % 2) * 64 + ((core + place // 128) % 2) * 32 + (place % 128) // 4
+    chosen = jnp.where(iota((128, 256), 0) == wanted, 1.0, 0.0).astype(BF16)
     precision_copy.wait()
     rep_ref[...] = jnp.dot(precision_ref[...], chosen, preferred_element_type=F32).astype(BF16)
 
 
-def sum_kernel(list_ref, b_ref, rep_ref, out_ref, lists_ref, hot_ref, w_ref, acc_ref, rows_ref):
-    lists_ref[...] = list_ref[...].T
-    number = iota((256, 256), 0).astype(F32).astype(BF16)
+def turn_kernel(list_ref, out_ref):
+    out_ref[...] = list_ref[...].T
+
+
+def sum_kernel(lists_ref, own_ref, other_ref, rep_ref, out_ref, hot_ref, w_ref, v_ref, acc_ref, rows_ref):
+    number = iota((256, 128), 0).astype(F32).astype(BF16)
     one, zero = jnp.ones((), BF16), jnp.zeros((), BF16)
     acc_ref[...] = jnp.zeros_like(acc_ref)
 
@@ -133,21 +138,21 @@
         for g in range(GROUPS):
             for c in range(4):
                 names = lists_ref[pl.ds(i * (4 * GROUPS) + g * 4 + c, 1), :].astype(BF16)
-                hot = jnp.where(number == jnp.broadcast_to(names, (256, 256)), one, zero)
-                hot_ref[g * 256 : (g + 1) * 256, c * 256 : (c + 1) * 256] = hot
+                hot = jnp.where(number == jnp.broadcast_to(names, (256, 128)), one, zero)
+                at = g * 512 + c * 128
+                hot_ref[:, at : at + 128] = hot
             rep = rep_ref[pl.ds(pl.multiple_of(i * (32 * GROUPS) + g * 32, 32), 32), :]
-            for f in range(8):
-                w_ref[f * 32 : (f + 1) * 32, g * 256 : (g + 1) * 256] = jnp.where(
-                    iota((32, 256), 1) % 8 == f, rep.astype(F32), 0.0
+            for f in range(4):
+                w_ref[g * 128 + f * 32 : g * 128 + (f + 1) * 32, :] = jnp.where(
+                    iota((32, 256), 1) % 4 == f, rep.astype(F32), 0.0
                 ).astype(BF16)
-        for n in range(2):
-            s = jnp.dot(hot_ref[...], b_ref[:, n * 512 : (n + 1) * 512], preferred_element_type=F32).astype(BF16)
-            for m in range(2):
-                wide = jnp.concatenate(
-                    [s[g * 256 : (g + 1) * 256, m * 256 : (m + 1) * 256] for g in range(GROUPS)], axis=1
-                )
-                cols = slice(n * 512 + m * 256, n * 512 + m * 256 + 256)
-                acc_ref[:, cols] += lax.dot_general(wide, w_ref[...], ANY_NT, preferred_element_type=F32)
+        for h in range(8):
+            cols = slice(h * 128, (h + 1) * 128)
+            both = jnp.concatenate([own_ref[:, cols], other_ref[:, cols]], axis=1)
+            v = lax.dot_general(both, w_ref[...], ANY_NT, preferred_element_type=F32).astype(BF16)
+            for g in range(GROUPS):
+                v_ref[g * 512 : (g + 1) * 512, cols] = v[:, g * 128 : (g + 1) * 128]
+        acc_ref[...] += jnp.dot(hot_ref[...], v_ref[...], preferred_element_type=F32)
         return carry
 
     lax.fori_loop(0, 32 // GROUPS, group, 0)
@@ -191,7 +196,7 @@
     block = jax.ShapeDtypeStruct((4, 8, 128), BF16)
     return pl.pallas_call(
         prepare_kernel,
-        out_shape=(jax.ShapeDtypeStruct((32, 8, 128), F32), block, block),
+        out_shape=(jax.ShapeDtypeStruct((16, 8, 128), F32), block, block),
         in_specs=anywhere(4),
         out_specs=tuple(vmem(3)),
         scratch_shapes=[
@@ -207,43 +212,56 @@
 
 
 def make_filtered(x, low, high, taps, precision):
+    half = jax.ShapeDtypeStruct((512, 1024), BF16)
     return pl.pallas_call(
         filter_kernel,
-        out_shape=(jax.ShapeDtypeStruct((1024, 1024), BF16), jax.ShapeDtypeStruct((1024, 256), BF16)),
+        out_shape=(half, half, jax.ShapeDtypeStruct((1024, 256), BF16)),
         in_specs=anywhere(1) + vmem(2) + anywhere(2),
-        out_specs=tuple(vmem(2)),
+        out_specs=tuple(vmem(3)),
         scratch_shapes=[
             pltpu.VMEM((4, 256, 8, 128), BF16),
             pltpu.VMEM((32, 129), BF16),
             pltpu.VMEM((32, 256), F32),
             pltpu.VMEM((1024, 128), BF16),
             pltpu.VMEM((2064, 128), F32),
-            pltpu.VMEM((16, 256, 128), F32),
+            pltpu.VMEM((32, 16, 2, 8, 128), F32),
             pltpu.SemaphoreType.DMA((6,)),
         ],
         compiler_params=params(51),
-        cost_estimate=pl.CostEstimate(flops=5_000_000_000, bytes_accessed=7_000_000, transcendentals=0),
+        cost_estimate=pl.CostEstimate(flops=15_000_000_000, bytes_accessed=7_000_000, transcendentals=0),
         name="make_filtered",
     )(x, low, high, taps, precision)
 
 
-def make_sums(lists, filtered, rep):
+def turn(lists):
+    return pl.pallas_call(
+        turn_kernel,
+        out_shape=jax.ShapeDtypeStruct((128, 128), F32),
+        in_specs=vmem(1),
+        out_specs=vmem(1)[0],
+        compiler_params=params(44),
+        cost_estimate=pl.CostEstimate(flops=40_000_000_000, bytes_accessed=130_000, transcendentals=0),
+        name="turn",
+    )(lists)
+
+
+def make_sums(lists, own, other, rep):
     return pl.pallas_call(
         sum_kernel,
         out_shape=jax.ShapeDtypeStruct((128, 16, 128), BF16),
-        in_specs=vmem(3),
+        in_specs=vmem(4),
         out_specs=vmem(1)[0],
         scratch_shapes=[
-            pltpu.VMEM((128, 256), F32),
-            pltpu.VMEM((GROUPS * 256, 1024), BF16),
-            pltpu.VMEM((256, GROUPS * 256), BF16),
+            pltpu.VMEM((256, GROUPS * 512), BF16),
+            pltpu.VMEM((GROUPS * 128, 256), BF16),
+            pltpu.VMEM((GROUPS * 512, 1024), BF16),
             pltpu.VMEM((256, 1024), F32),
             pltpu.VMEM((2048, 128), F32),
         ],
         compiler_params=params(44),
-        cost_estimate=pl.CostEstimate(flops=22_000_000_000, bytes_accessed=3_000_000, transcendentals=0),
+        cost_estimate=pl.CostEstimate(flops=17_000_000_000, bytes_accessed=3_000_000, transcendentals=0),
         name="make_sums",
-    )(lists, filtered, rep)
+    )(lists, own, other, rep)
 
 
 def make_tiles(received, left, right):
@@ -270,29 +288,25 @@
     own, first, last = prepare(frame_count.reshape(1, 1), frame_tile.reshape(8, 128), tile_owner.reshape(1, 256), x)
     low = lax.ppermute(last, "tm", forward)
     high = lax.ppermute(first, "tm", backward)
-    lists = lax.all_to_all(own, "det", split_axis=0, concat_axis=0, tiled=True)
-    filtered, rep = make_filtered(x, low, high, filter_taps, det_precision)
-    sums = make_sums(lists.reshape(256, 128), filtered, rep)
-    received = lax.all_to_all(sums, ("tm", "det"), split_axis=0, concat_axis=0, tiled=True)
+    lists = lax.all_to_all(own, "chip", split_axis=0, concat_axis=0, tiled=True)
+    kept, sent, rep = make_filtered(x, low, high, filter_taps, det_precision)
+    other = lax.ppermute(sent, "core", [(0, 1), (1, 0)])
+    sums = make_sums(turn(lists.reshape(128, 128)), kept, other, rep)
+    received = lax.all_to_all(sums, ("tm", "chip", "core"), split_axis=0, concat_axis=0, tiled=True)
     right = right_weight.reshape(128, 8, 4).transpose(2, 1, 0).reshape(32, 128)
     tiles = make_tiles(received, left_weight.T, right)
     return tiles.reshape(128, 2, 128).transpose(1, 0, 2).reshape(2, 16384)
 
 
 def solution(mesh):
+    devices = mesh.devices
+    split = jax.sharding.Mesh(devices.reshape(devices.shape[0], -1, 2), ("tm", "chip", "core"))
+    det = ("chip", "core")
+    every = ("tm", "chip", "core")
     return jax.shard_map(
         local,
-        mesh=mesh,
-        in_specs=(
-            P("det", "tm"),
-            P("det", None),
-            P(),
-            P(),
-            P(),
-            P(("tm", "det"), None),
-            P(),
-            P(("tm", "det")),
-        ),
-        out_specs=P(("tm", "det"), None),
+        mesh=split,
+        in_specs=(P(det, "tm"), P(det, None), P(), P(), P(), P(every, None), P(), P(every)),
+        out_specs=P(every, None),
         check_vma=False,
     )

time: 70.4 us -> 72.7 us (1.033)
  waiting for transfers between devices: 14.2 us -> 15.9 us
  Pallas kernels: 34.6 us -> 33.7 us
  local copies, waits for them, and re-layouts: 0.01 us -> 0.81 us
    ppermute x0 -> x1, waiting for transfers between devices: none -> 2.19 us  [local(): other = lax.ppermute(sent, 'core', [(0, 1), (1, 0)])]
    pallas_call x1, Pallas kernels: 23.7 us -> 22.4 us  [make_sums(): pl.pallas_call(sum_kernel, out_shape=jax.ShapeDtypeStruct((128, 16, 128),...]
    ppermute x0 -> x1, starting transfers between devices: none -> 1.24 us  [local(): other = lax.ppermute(sent, 'core', [(0, 1), (1, 0)])]
    unnamed x6 -> x10, local copies, waits for them, and re-layouts: 0.01 us -> 0.8 us
    pallas_call x2 -> x3, Pallas kernels: 9.15 us -> 9.51 us  [the longest x1 7.4 us: make_filtered(): pl.pallas_call(filter_kernel, out_shape=(half, half, jax.ShapeDtypeStruct...]
  transfers between devices with their start and end apart: 4 -> 5, of which waited for: 2 -> 2; matrix products, arithmetic and copies ran while one was open for 0% -> 0% of each run, Pallas kernels for 10% -> 10%
where the time goes in v4:
time: 72.7 us; the launch traced here: 72.4 us
  Pallas kernels  33.7 us (46%)
  starting transfers between devices  21.2 us (29%)
  waiting for transfers between devices  15.9 us (22%)
  local copies, waits for them, and re-layouts  0.81 us (1%)
  between operations  0.75 us (1%)
    pallas_call x1, Pallas kernels, make_sums(): pl.pallas_call(sum_kernel, out_shape=jax.ShapeDtypeStruct((128, 16, 128),...  22.4 us
    all_to_all x1, waiting for transfers between devices, local(): lax.all_to_all(sums, ('tm', 'chip', 'core'), split_axis=0, concat_axis=0,...  13.7 us
    all_to_all x1, starting transfers between devices, local(): lax.all_to_all(sums, ('tm', 'chip', 'core'), split_axis=0, concat_axis=0,...  8.46 us
    pallas_call x1, Pallas kernels, make_filtered(): pl.pallas_call(filter_kernel, out_shape=(half, half, jax.ShapeDtypeStruct...  7.4 us
    all_to_all x1, starting transfers between devices, local(): lists = lax.all_to_all(own, 'chip', split_axis=0, concat_axis=0, tiled=True)  6.75 us
    ppermute x1, starting transfers between devices, local(): low = lax.ppermute(last, 'tm', forward)  2.54 us
    ppermute x1, starting transfers between devices, local(): high = lax.ppermute(first, 'tm', backward)  2.2 us
    ppermute x1, waiting for transfers between devices, local(): other = lax.ppermute(sent, 'core', [(0, 1), (1, 0)])  2.19 us
  transfers between devices with their start and end apart: 5, of which 2 were waited for; matrix products, arithmetic and copies ran while one was open for 0% of the time, Pallas kernels for 10%

profile of v4, /device:TPU:1, one launch (start us, length us, event | category | flops | bytes accessed | tf_op | source)
XLA Modules:
  0.0 72.4 jit_solution(13843352799178932695)
XLA Ops:
  0.0 0.0 copy-start.1
  0.7 2.0 %prepare.1 = (f32[16,8,128]{2,1,0:T(8,128)}, bf16[4,8,128]{2,1,0:T(8,128)(2,1)}, bf16[4,8,128]{2,1,0:T(8,128)(2,1)}) custom-call(s32[1,1]{1,0:T(1,128)} %bitcast.19.count_hbm, s32[8,128]{1,0:T(8,128)} %bitcast.26, s32[1,256]{1,0:T(1,128)} %bitcast.27, bf16[4,256,8,128]{3,2,1,0:T(8,128)(2,1)} %bitcast.23), custom_call_target="tpu_custom_call" | custom-call | flops 4000000 | bytes 200000 | tf_op jit(solution)/shard_map/prepare/pallas_call | solution.py:197
  2.7 2.5 %collective-permute-start = (bf16[4,8,128]{2,1,0:T(8,128)(2,1)}, bf16[4,8,128]{2,1,0:T(8,128)(2,1)S(1)}, u32[]{:S(2)}, u32[]{:S(2)}) collective-permute-start(bf16[4,8,128]{2,1,0:T(8,128)(2,1)} %get-tuple-element.12), channel_id=1, source_target_pairs={{0,32},{32,64},{64,96},{96,0},{1,33},{33,65},{65,97},{97,1},{2,34}... | collective-permute-start | bytes 24584 | tf_op jit(solution)/shard_map/ppermute | solution.py:289
  5.2 2.2 %collective-permute-start.1 = (bf16[4,8,128]{2,1,0:T(8,128)(2,1)}, bf16[4,8,128]{2,1,0:T(8,128)(2,1)S(1)}, u32[]{:S(2)}, u32[]{:S(2)}) collective-permute-start(bf16[4,8,128]{2,1,0:T(8,128)(2,1)} %get-tuple-element.13), channel_id=1, source_target_pairs={{32,0},{64,32},{96,64},{0,96},{33,1},{65,33},{97,65},{1,97},{34,2}... | collective-permute-start | bytes 24584 | tf_op jit(solution)/shard_map/ppermute | solution.py:290
  7.4 6.8 %all-to-all-start = ((f32[16,8,128]{2,1,0:T(8,128)}), f32[16,8,128]{2,1,0:T(8,128)S(1)}, u32[]{:S(2)}, u32[]{:S(2)}) async-start(f32[16,8,128]{2,1,0:T(8,128)} %get-tuple-element.11), calls=%async_computation | async-start | bytes 131072 | tf_op jit(solution)/shard_map/all_to_all | solution.py:291
  14.2 0.0 collective-permute-done.low_ref
  14.2 0.0 collective-permute-done.1.high_ref
  14.2 0.0 copy-done.1
  14.2 7.4 %make_filtered.1 = (bf16[512,1024]{1,0:T(8,128)(2,1)S(1)}, bf16[512,1024]{1,0:T(8,128)(2,1)S(1)}, bf16[1024,256]{1,0:T(8,128)(2,1)S(1)}) custom-call(bf16[4,256,8,128]{3,2,1,0:T(8,128)(2,1)} %bitcast.24, bf16[4,8,128]{2,1,0:T(8,128)(2,1)S(1)} %collective-permute-done.low_ref, bf16[4,8,128]{2,1,0:T(8,128)(2,1)S(1)} %collective-permute-done.1.high_ref, ...), custom_call_target="tpu_custom_call" | custom-call | flops 15000000512 | bytes 7000000 | tf_op jit(solution)/shard_map/make_filtered/pallas_call | solution.py:216
  21.6 0.0 copy-start.2
  21.6 0.8 %copy-done.2 = bf16[1024,256]{1,0:T(8,128)(2,1)} copy-done((bf16[1024,256]{1,0:T(8,128)(2,1)}, bf16[1024,256]{1,0:T(8,128)(2,1)S(1)}, u32[]{:S(2)}) %copy-start.2) | copy-done | bytes 524312
  22.4 1.2 %collective-permute-start.2 = (bf16[512,1024]{1,0:T(8,128)(2,1)S(1)}, bf16[512,1024]{1,0:T(8,128)(2,1)S(1)}, u32[]{:S(2)}, u32[]{:S(2)}) collective-permute-start(bf16[512,1024]{1,0:T(8,128)(2,1)S(1)} %get-tuple-element.15), channel_id=1, source_target_pairs={{0,1},{1,0},{2,3},{3,2},{4,5},{5,4},{6,7},{7,6},{8,9},{9,8},{10,11... | collective-permute-start | bytes 3145736 | tf_op jit(solution)/shard_map/ppermute | solution.py:293
  23.7 0.0 all-to-all-done
  23.7 0.0 copy-start.3
  23.7 0.1 turn.1.lists_ref
  23.8 2.2 %collective-permute-done.2.other_ref = bf16[512,1024]{1,0:T(8,128)(2,1)S(1)} collective-permute-done((bf16[512,1024]{1,0:T(8,128)(2,1)S(1)}, bf16[512,1024]{1,0:T(8,128)(2,1)S(1)}, u32[]{:S(2)}, u32[]{:S(2)}) %collective-permute-start.2) | collective-permute-done | bytes 1048608 | tf_op jit(solution)/shard_map/ppermute | solution.py:293
  26.0 0.0 copy-done.3
  26.0 0.0 copy-start.4
  26.0 0.0 copy-start
  26.0 22.4 %make_sums.1 = bf16[128,16,128]{2,1,0:T(8,128)(2,1)} custom-call(f32[128,128]{1,0:T(8,128)S(1)} %turn.1.lists_ref, bf16[512,1024]{1,0:T(8,128)(2,1)S(1)} %get-tuple-element.14.own_ref, bf16[512,1024]{1,0:T(8,128)(2,1)S(1)} %collective-permute-done.2.other_ref, bf16[1024,256]{1,0:T(8,128)(2,1)S(1)} %copy-done.3), custom_call_target="tpu_custom_call" | custom-call | flops 16999999488 | bytes 3000000 | tf_op jit(solution)/shard_map/make_sums/pallas_call | solution.py:249
  48.4 8.5 %all-to-all-start.1 = ((bf16[128,16,128]{2,1,0:T(8,128)(2,1)}), bf16[128,16,128]{2,1,0:T(8,128)(2,1)S(1)}, u32[]{:S(2)}, u32[]{:S(2)}) async-start(bf16[128,16,128]{2,1,0:T(8,128)(2,1)} %make_sums.1), calls=%async_computation.1 | async-start | bytes 1048576 | tf_op jit(solution)/shard_map/all_to_all | solution.py:295
  56.9 0.0 copy-done.4
  56.9 13.7 %all-to-all-done.1.in_ref = bf16[128,16,128]{2,1,0:T(8,128)(2,1)S(1)} async-done(((bf16[128,16,128]{2,1,0:T(8,128)(2,1)}), bf16[128,16,128]{2,1,0:T(8,128)(2,1)S(1)}, u32[]{:S(2)}, u32[]{:S(2)}) %all-to-all-start.1) | async-done | bytes 524320 | tf_op jit(solution)/shard_map/all_to_all | solution.py:295
  70.6 0.0 copy-done
  70.6 1.8 %make_tiles.1 = f32[256,128]{1,0:T(8,128)} custom-call(bf16[128,16,128]{2,1,0:T(8,128)(2,1)S(1)} %all-to-all-done.1.in_ref, f32[32,128]{1,0:T(8,128)S(1)} %bitcast.22, f32[32,128]{1,0:T(8,128)S(1)} %bitcast.20), custom_call_target="tpu_custom_call" | custom-call | flops 40000000 | bytes 700000 | tf_op jit(solution)/shard_map/make_tiles/pallas_call | solution.py:268
  (1 shorter events, 0.0 us)
Async XLA Ops:
  0.0 14.2 %copy-start.1 = (bf16[32,129]{1,0:T(8,128)(2,1)S(1)}, bf16[32,129]{1,0:T(8,128)(2,1)}, u32[]{:S(2)}) copy-start(bf16[32,129]{1,0:T(8,128)(2,1)} %taps_hbm.1) | copy-start | bytes 24772
  2.7 11.5 %collective-permute-start = (bf16[4,8,128]{2,1,0:T(8,128)(2,1)}, bf16[4,8,128]{2,1,0:T(8,128)(2,1)S(1)}, u32[]{:S(2)}, u32[]{:S(2)}) collective-permute-start(bf16[4,8,128]{2,1,0:T(8,128)(2,1)} %get-tuple-element.12), channel_id=1, source_target_pairs={{0,32},{32,64},{64,96},{96,0},{1,33},{33,65},{65,97},{97,1},{2,34}... | collective-permute-start | bytes 24584 | tf_op jit(solution)/shard_map/ppermute | solution.py:289
  5.2 9.0 %collective-permute-start.1 = (bf16[4,8,128]{2,1,0:T(8,128)(2,1)}, bf16[4,8,128]{2,1,0:T(8,128)(2,1)S(1)}, u32[]{:S(2)}, u32[]{:S(2)}) collective-permute-start(bf16[4,8,128]{2,1,0:T(8,128)(2,1)} %get-tuple-element.13), channel_id=1, source_target_pairs={{32,0},{64,32},{96,64},{0,96},{33,1},{65,33},{97,65},{1,97},{34,2}... | collective-permute-start | bytes 24584 | tf_op jit(solution)/shard_map/ppermute | solution.py:290
  7.4 16.2 %all-to-all-start = ((f32[16,8,128]{2,1,0:T(8,128)}), f32[16,8,128]{2,1,0:T(8,128)S(1)}, u32[]{:S(2)}, u32[]{:S(2)}) async-start(f32[16,8,128]{2,1,0:T(8,128)} %get-tuple-element.11), calls=%async_computation | async-start | bytes 131072 | tf_op jit(solution)/shard_map/all_to_all | solution.py:291
  21.6 0.8 %copy-start.2 = (bf16[1024,256]{1,0:T(8,128)(2,1)}, bf16[1024,256]{1,0:T(8,128)(2,1)S(1)}, u32[]{:S(2)}) copy-start(bf16[1024,256]{1,0:T(8,128)(2,1)S(1)} %get-tuple-element.16.rep_ref) | copy-start | bytes 1572868
  22.4 3.5 %collective-permute-start.2 = (bf16[512,1024]{1,0:T(8,128)(2,1)S(1)}, bf16[512,1024]{1,0:T(8,128)(2,1)S(1)}, u32[]{:S(2)}, u32[]{:S(2)}) collective-permute-start(bf16[512,1024]{1,0:T(8,128)(2,1)S(1)} %get-tuple-element.15), channel_id=1, source_target_pairs={{0,1},{1,0},{2,3},{3,2},{4,5},{5,4},{6,7},{7,6},{8,9},{9,8},{10,11... | collective-permute-start | bytes 3145736 | tf_op jit(solution)/shard_map/ppermute | solution.py:293
  23.7 2.3 %copy-start.3 = (bf16[1024,256]{1,0:T(8,128)(2,1)S(1)}, bf16[1024,256]{1,0:T(8,128)(2,1)}, u32[]{:S(2)}) copy-start(bf16[1024,256]{1,0:T(8,128)(2,1)} %copy-done.2) | copy-start | bytes 1572868
  26.0 30.9 %copy-start.4 = (f32[128,32]{0,1:T(8,128)S(1)}, f32[128,32]{0,1:T(8,128)}, u32[]{:S(2)}) copy-start(f32[128,32]{0,1:T(8,128)} %param.12) | copy-start | bytes 49156
  26.0 44.6 %copy-start = (f32[128,32]{0,1:T(8,128)S(1)}, f32[128,32]{0,1:T(8,128)}, u32[]{:S(2)}) copy-start(f32[128,32]{0,1:T(8,128)} %param.11) | copy-start | bytes 49156
  48.4 22.2 %all-to-all-start.1 = ((bf16[128,16,128]{2,1,0:T(8,128)(2,1)}), bf16[128,16,128]{2,1,0:T(8,128)(2,1)S(1)}, u32[]{:S(2)}, u32[]{:S(2)}) async-start(bf16[128,16,128]{2,1,0:T(8,128)(2,1)} %make_sums.1), calls=%async_computation.1 | async-start | bytes 1048576 | tf_op jit(solution)/shard_map/all_to_all | solution.py:295

commit v5 on v3

--- a/solution.py
+++ b/solution.py
@@ -22,7 +22,7 @@
     return pltpu.CompilerParams(vmem_limit_bytes=mib << 20)
 
 
-def prepare_kernel(count_hbm, tile_hbm, owner_hbm, x_hbm, out_ref, first_ref, last_ref, count_ref, tile_ref, owner_ref, sems):
+def prepare_kernel(count_hbm, tile_hbm, owner_hbm, x_hbm, out_ref, first_ref, last_ref, count_ref, tile_ref, owner_ref, order_ref, sems):
     copies = [
         pltpu.make_async_copy(count_hbm, count_ref, sems.at[0]),
         pltpu.make_async_copy(tile_hbm, tile_ref, sems.at[1]),
@@ -32,10 +32,13 @@
     ]
     for copy in copies:
         copy.start()
-    for copy in copies:
+    lane, place = iota((128, 1024), 0), iota((128, 1024), 1)
+    wanted = ((place % 16) // 4) * 32 + (place // 128) * 4 + place % 4
+    order_ref[...] = jnp.where(lane == wanted, 1.0, 0.0).astype(BF16)
+    row, col = iota((256, 256), 0), iota((256, 256), 1)
+    for copy in copies[:3]:
         copy.wait()
     owner = owner_ref[...]
-    row, col = iota((256, 256), 0), iota((256, 256), 1)
     owner_col = jnp.sum(jnp.where(row == col, owner, 0), axis=1, keepdims=True)
     rank = jnp.sum(jnp.where((owner_col == owner) & (col < row), 1, 0), axis=1, keepdims=True)
     dest_col = owner_col * 2 + rank
@@ -47,15 +50,15 @@
         dest = jnp.sum(jnp.where(number == tile, dest_col, 0), axis=0, keepdims=True)
         rows.append(jnp.where(iota((1, 128), 1) + r * 128 < count, dest, 256))
     natural = jnp.concatenate(rows, axis=0).astype(F32).astype(BF16)
-    lane, place = iota((128, 1024), 0), iota((128, 1024), 1)
-    wanted = ((place % 16) // 4) * 32 + (place // 128) * 4 + place % 4
-    spread = jnp.dot(natural, jnp.where(lane == wanted, 1.0, 0.0).astype(BF16), preferred_element_type=F32)
+    spread = jnp.dot(natural, order_ref[...], preferred_element_type=F32)
     mine = iota((8, 128), 0) == iota((8, 128), 1) // 16
     picked = [
         jnp.sum(jnp.where(mine, spread[:, c * 128 : (c + 1) * 128], 0.0), axis=0, keepdims=True)
         for c in range(8)
     ]
     out_ref[...] = jnp.broadcast_to(jnp.concatenate(picked, axis=0)[None], out_ref.shape)
+    for copy in copies[3:]:
+        copy.wait()
 
 
 def butterfly(arrays, chunk):
@@ -74,7 +77,7 @@
 
 def filter_kernel(
     x_hbm, low_ref, high_ref, taps_hbm, precision_hbm, b_ref, rep_ref,
-    x_ref, narrow_ref, taps_ref, precision_ref, rows_ref, y_ref, sems,
+    x_ref, narrow_ref, taps_ref, precision_ref, matrix_ref, rows_ref, y_ref, sems,
 ):
     taps_copy = pltpu.make_async_copy(taps_hbm, narrow_ref, sems.at[0])
     taps_copy.start()
@@ -93,6 +96,9 @@
     tm = lax.axis_index("tm")
     has_low = jnp.where(tm > 0, 1.0, 0.0)
     has_high = jnp.where(tm < lax.axis_size("tm") - 1, 1.0, 0.0)
+    for d in range(32):
+        taps = jnp.broadcast_to(taps_ref[d : d + 1, :], (128, 256))
+        matrix_ref[d] = pltpu.roll(taps, 192, 1, stride=1, stride_axis=0).astype(BF16)
     for half in range(2):
         for g in range(2):
             dg = half * 2 + g
@@ -105,9 +111,9 @@
                 here = rows_ref[pl.ds(8 + d, 256, stride=8), :]
                 after = rows_ref[pl.ds(16 + d, 256, stride=8), :]
                 window = jnp.concatenate([here, jnp.where(first_half, after, before)], axis=1).astype(BF16)
-                taps = jnp.broadcast_to(taps_ref[dg * 8 + d : dg * 8 + d + 1, :], (128, 256))
-                matrix = pltpu.roll(taps, 192, 1, stride=1, stride_axis=0).astype(BF16)
-                y_ref[g * 8 + d] = lax.dot_general(window, matrix, ANY_NT, preferred_element_type=F32)
+                y_ref[g * 8 + d] = lax.dot_general(
+                    window, matrix_ref[dg * 8 + d], ANY_NT, preferred_element_type=F32
+                )
 
         def chunk(i, carry):
             at = pl.multiple_of(i * 128, 128)
@@ -161,18 +167,10 @@
     left = left_ref[...]
     wide = jnp.concatenate([left] * 4, axis=0)
     lane_group = iota((128, 128), 0) // 32
+    spread = jnp.concatenate([jnp.where(lane_group == q, wide, 0.0) for q in range(4)], axis=1)
+    parts = jnp.dot(total, spread, precision=lax.Precision.HIGHEST, preferred_element_type=F32)
     for t in range(2):
-        frame = total[t * 8 : (t + 1) * 8]
-        parts = [
-            jnp.dot(
-                frame,
-                jnp.where(lane_group == q, wide, 0.0),
-                precision=lax.Precision.HIGHEST,
-                preferred_element_type=F32,
-            )
-            for q in range(4)
-        ]
-        mixed = jnp.concatenate(parts, axis=0)
+        mixed = jnp.concatenate([parts[t * 8 : (t + 1) * 8, q * 128 : (q + 1) * 128] for q in range(4)], axis=0)
         tile = lax.dot_general(
             mixed, right_ref[...], TN, precision=lax.Precision.HIGHEST, preferred_element_type=F32
         )
@@ -198,6 +196,7 @@
             pltpu.VMEM((1, 1), jnp.int32),
             pltpu.VMEM((8, 128), jnp.int32),
             pltpu.VMEM((1, 256), jnp.int32),
+            pltpu.VMEM((128, 1024), BF16),
             pltpu.SemaphoreType.DMA((5,)),
         ],
         compiler_params=params(60),
@@ -217,6 +216,7 @@
             pltpu.VMEM((32, 129), BF16),
             pltpu.VMEM((32, 256), F32),
             pltpu.VMEM((1024, 128), BF16),
+            pltpu.VMEM((32, 128, 256), BF16),
             pltpu.VMEM((2064, 128), F32),
             pltpu.VMEM((16, 256, 128), F32),
             pltpu.SemaphoreType.DMA((6,)),

time: 70.4 us -> 69.6 us (0.989)
  Pallas kernels: 34.6 us -> 33.8 us
where the time goes in v5:
time: 69.6 us; the launch traced here: 69.3 us
  Pallas kernels  33.8 us (49%)
  starting transfers between devices  20.2 us (29%)
  waiting for transfers between devices  14.5 us (21%)
  between operations  0.74 us (1%)
    pallas_call x1, Pallas kernels, make_sums(): pl.pallas_call(sum_kernel, out_shape=jax.ShapeDtypeStruct((128, 16, 128),...  23.7 us
    all_to_all x1, waiting for transfers between devices, local(): lax.all_to_all(sums, ('tm', 'det'), split_axis=0, concat_axis=0, tiled=True)  13.7 us
    all_to_all x1, starting transfers between devices, local(): lists = lax.all_to_all(own, 'det', split_axis=0, concat_axis=0, tiled=True)  8.04 us
    all_to_all x1, starting transfers between devices, local(): lax.all_to_all(sums, ('tm', 'det'), split_axis=0, concat_axis=0, tiled=True)  7.47 us
    pallas_call x1, Pallas kernels, make_filtered(): pl.pallas_call(filter_kernel, out_shape=(jax.ShapeDtypeStruct((1024, 1024...  6.84 us
    ppermute x1, starting transfers between devices, local(): low = lax.ppermute(last, 'tm', forward)  2.54 us
    ppermute x1, starting transfers between devices, local(): high = lax.ppermute(first, 'tm', backward)  2.2 us
    pallas_call x1, Pallas kernels, prepare(): pl.pallas_call(prepare_kernel, out_shape=(jax.ShapeDtypeStruct((32, 8, 12...  1.98 us
  transfers between devices with their start and end apart: 4, of which 2 were waited for; matrix products, arithmetic and copies ran while one was open for 0% of the time, Pallas kernels for 10%

profile of v5, /device:TPU:1, one launch (start us, length us, event | category | flops | bytes accessed | tf_op | source)
XLA Modules:
  0.0 69.3 jit_solution(305831918031677054)
XLA Ops:
  0.0 0.0 copy-start.1
  0.7 2.0 %prepare.1 = (f32[32,8,128]{2,1,0:T(8,128)}, bf16[4,8,128]{2,1,0:T(8,128)(2,1)}, bf16[4,8,128]{2,1,0:T(8,128)(2,1)}) custom-call(s32[1,1]{1,0:T(1,128)} %bitcast.19.count_hbm, s32[8,128]{1,0:T(8,128)} %bitcast.26, s32[1,256]{1,0:T(1,128)} %bitcast.27, bf16[4,256,8,128]{3,2,1,0:T(8,128)(2,1)} %bitcast.23), custom_call_target="tpu_custom_call" | custom-call | flops 4000000 | bytes 200000 | tf_op jit(solution)/shard_map/prepare/pallas_call | solution.py:190
  2.6 2.5 %collective-permute-start = (bf16[4,8,128]{2,1,0:T(8,128)(2,1)}, bf16[4,8,128]{2,1,0:T(8,128)(2,1)S(1)}, u32[]{:S(2)}, u32[]{:S(2)}) collective-permute-start(bf16[4,8,128]{2,1,0:T(8,128)(2,1)} %get-tuple-element.11), channel_id=1, source_target_pairs={{0,32},{32,64},{64,96},{96,0},{1,33},{33,65},{65,97},{97,1},{2,34}... | collective-permute-start | bytes 24584 | tf_op jit(solution)/shard_map/ppermute | solution.py:271
  5.2 2.2 %collective-permute-start.1 = (bf16[4,8,128]{2,1,0:T(8,128)(2,1)}, bf16[4,8,128]{2,1,0:T(8,128)(2,1)S(1)}, u32[]{:S(2)}, u32[]{:S(2)}) collective-permute-start(bf16[4,8,128]{2,1,0:T(8,128)(2,1)} %get-tuple-element.12), channel_id=1, source_target_pairs={{32,0},{64,32},{96,64},{0,96},{33,1},{65,33},{97,65},{1,97},{34,2}... | collective-permute-start | bytes 24584 | tf_op jit(solution)/shard_map/ppermute | solution.py:272
  7.4 8.0 %all-to-all-start = ((f32[32,8,128]{2,1,0:T(8,128)}), f32[32,8,128]{2,1,0:T(8,128)S(1)}, u32[]{:S(2)}, u32[]{:S(2)}) async-start(f32[32,8,128]{2,1,0:T(8,128)} %get-tuple-element.10), calls=%async_computation | async-start | bytes 262144 | tf_op jit(solution)/shard_map/all_to_all | solution.py:273
  15.4 0.0 collective-permute-done.low_ref
  15.4 0.0 collective-permute-done.1.high_ref
  15.5 0.0 copy-done.1
  15.5 6.8 %make_filtered.1 = (bf16[1024,1024]{1,0:T(8,128)(2,1)S(1)}, bf16[1024,256]{1,0:T(8,128)(2,1)S(1)}) custom-call(bf16[4,256,8,128]{3,2,1,0:T(8,128)(2,1)} %bitcast.24, bf16[4,8,128]{2,1,0:T(8,128)(2,1)S(1)} %collective-permute-done.low_ref, bf16[4,8,128]{2,1,0:T(8,128)(2,1)S(1)} %collective-permute-done.1.high_ref, bf16[32,129]{1,0:T(8,128)(2,1)S(1)} %copy-done.1, ...), custom_call_target="tpu_custom_call" | custom-call | flops 5000000000 | bytes 7000000 | tf_op jit(solution)/shard_map/make_filtered/pallas_call | solution.py:209
  22.3 0.8 %all-to-all-done = f32[32,8,128]{2,1,0:T(8,128)S(1)} async-done(((f32[32,8,128]{2,1,0:T(8,128)}), f32[32,8,128]{2,1,0:T(8,128)S(1)}, u32[]{:S(2)}, u32[]{:S(2)}) %all-to-all-start) | async-done | bytes 131104 | tf_op jit(solution)/shard_map/all_to_all | solution.py:273
  23.1 0.0 copy-start.2
  23.1 0.0 copy-start
  23.1 23.7 %make_sums.1 = bf16[128,16,128]{2,1,0:T(8,128)(2,1)} custom-call(f32[256,128]{1,0:T(8,128)S(1)} %bitcast.20, bf16[1024,1024]{1,0:T(8,128)(2,1)S(1)} %get-tuple-element.13.b_ref, bf16[1024,256]{1,0:T(8,128)(2,1)S(1)} %get-tuple-element.14.rep_ref), custom_call_target="tpu_custom_call" | custom-call | flops 22000001024 | bytes 3000000 | tf_op jit(solution)/shard_map/make_sums/pallas_call | solution.py:231
  46.8 7.5 %all-to-all-start.1 = ((bf16[128,16,128]{2,1,0:T(8,128)(2,1)}), bf16[128,16,128]{2,1,0:T(8,128)(2,1)S(1)}, u32[]{:S(2)}, u32[]{:S(2)}) async-start(bf16[128,16,128]{2,1,0:T(8,128)(2,1)} %make_sums.1), calls=%async_computation.1 | async-start | bytes 1048576 | tf_op jit(solution)/shard_map/all_to_all | solution.py:276
  54.3 0.0 copy-done.2
  54.3 13.7 %all-to-all-done.1.in_ref = bf16[128,16,128]{2,1,0:T(8,128)(2,1)S(1)} async-done(((bf16[128,16,128]{2,1,0:T(8,128)(2,1)}), bf16[128,16,128]{2,1,0:T(8,128)(2,1)S(1)}, u32[]{:S(2)}, u32[]{:S(2)}) %all-to-all-start.1) | async-done | bytes 524320 | tf_op jit(solution)/shard_map/all_to_all | solution.py:276
  68.0 0.0 copy-done
  68.0 1.3 %make_tiles.1 = f32[256,128]{1,0:T(8,128)} custom-call(bf16[128,16,128]{2,1,0:T(8,128)(2,1)S(1)} %all-to-all-done.1.in_ref, f32[32,128]{1,0:T(8,128)S(1)} %bitcast.22, f32[32,128]{1,0:T(8,128)S(1)} %bitcast.21), custom_call_target="tpu_custom_call" | custom-call | flops 40000000 | bytes 700000 | tf_op jit(solution)/shard_map/make_tiles/pallas_call | solution.py:250
  (1 shorter events, 0.0 us)
Async XLA Ops:
  0.0 15.5 %copy-start.1 = (bf16[32,129]{1,0:T(8,128)(2,1)S(1)}, bf16[32,129]{1,0:T(8,128)(2,1)}, u32[]{:S(2)}) copy-start(bf16[32,129]{1,0:T(8,128)(2,1)} %taps_hbm.1) | copy-start | bytes 24772
  2.6 12.8 %collective-permute-start = (bf16[4,8,128]{2,1,0:T(8,128)(2,1)}, bf16[4,8,128]{2,1,0:T(8,128)(2,1)S(1)}, u32[]{:S(2)}, u32[]{:S(2)}) collective-permute-start(bf16[4,8,128]{2,1,0:T(8,128)(2,1)} %get-tuple-element.11), channel_id=1, source_target_pairs={{0,32},{32,64},{64,96},{96,0},{1,33},{33,65},{65,97},{97,1},{2,34}... | collective-permute-start | bytes 24584 | tf_op jit(solution)/shard_map/ppermute | solution.py:271
  5.2 10.3 %collective-permute-start.1 = (bf16[4,8,128]{2,1,0:T(8,128)(2,1)}, bf16[4,8,128]{2,1,0:T(8,128)(2,1)S(1)}, u32[]{:S(2)}, u32[]{:S(2)}) collective-permute-start(bf16[4,8,128]{2,1,0:T(8,128)(2,1)} %get-tuple-element.12), channel_id=1, source_target_pairs={{32,0},{64,32},{96,64},{0,96},{33,1},{65,33},{97,65},{1,97},{34,2}... | collective-permute-start | bytes 24584 | tf_op jit(solution)/shard_map/ppermute | solution.py:272
  7.4 15.7 %all-to-all-start = ((f32[32,8,128]{2,1,0:T(8,128)}), f32[32,8,128]{2,1,0:T(8,128)S(1)}, u32[]{:S(2)}, u32[]{:S(2)}) async-start(f32[32,8,128]{2,1,0:T(8,128)} %get-tuple-element.10), calls=%async_computation | async-start | bytes 262144 | tf_op jit(solution)/shard_map/all_to_all | solution.py:273
  23.1 31.2 %copy-start.2 = (f32[128,32]{0,1:T(8,128)S(1)}, f32[128,32]{0,1:T(8,128)}, u32[]{:S(2)}) copy-start(f32[128,32]{0,1:T(8,128)} %param.12) | copy-start | bytes 49156
  23.1 44.9 %copy-start = (f32[128,32]{0,1:T(8,128)S(1)}, f32[128,32]{0,1:T(8,128)}, u32[]{:S(2)}) copy-start(f32[128,32]{0,1:T(8,128)} %param.11) | copy-start | bytes 49156
  46.8 21.2 %all-to-all-start.1 = ((bf16[128,16,128]{2,1,0:T(8,128)(2,1)}), bf16[128,16,128]{2,1,0:T(8,128)(2,1)S(1)}, u32[]{:S(2)}, u32[]{:S(2)}) async-start(bf16[128,16,128]{2,1,0:T(8,128)(2,1)} %make_sums.1), calls=%async_computation.1 | async-start | bytes 1048576 | tf_op jit(solution)/shard_map/all_to_all | solution.py:276

commit v6 on v5

--- a/solution.py
+++ b/solution.py
@@ -10,7 +10,7 @@
 F32 = jnp.float32
 BF16 = jnp.bfloat16
 ANY_NT = (((1,), (1,)), ((), ()))
-GROUPS = 8
+GROUPS = 4
 TN = (((0,), (0,)), ((), ()))
 
 
@@ -133,30 +133,30 @@
     lists_ref[...] = list_ref[...].T
     number = iota((256, 256), 0).astype(F32).astype(BF16)
     one, zero = jnp.ones((), BF16), jnp.zeros((), BF16)
-    acc_ref[...] = jnp.zeros_like(acc_ref)
-
-    def group(i, carry):
+
+    def group(i):
         for g in range(GROUPS):
             for c in range(4):
                 names = lists_ref[pl.ds(i * (4 * GROUPS) + g * 4 + c, 1), :].astype(BF16)
                 hot = jnp.where(number == jnp.broadcast_to(names, (256, 256)), one, zero)
-                hot_ref[g * 256 : (g + 1) * 256, c * 256 : (c + 1) * 256] = hot
+                hot_ref[i % 2, g * 256 : (g + 1) * 256, c * 256 : (c + 1) * 256] = hot
             rep = rep_ref[pl.ds(pl.multiple_of(i * (32 * GROUPS) + g * 32, 32), 32), :]
             for f in range(8):
-                w_ref[f * 32 : (f + 1) * 32, g * 256 : (g + 1) * 256] = jnp.where(
+                w_ref[i % 2, f * 32 : (f + 1) * 32, g * 256 : (g + 1) * 256] = jnp.where(
                     iota((32, 256), 1) % 8 == f, rep.astype(F32), 0.0
                 ).astype(BF16)
         for n in range(2):
-            s = jnp.dot(hot_ref[...], b_ref[:, n * 512 : (n + 1) * 512], preferred_element_type=F32).astype(BF16)
+            s = jnp.dot(hot_ref[i % 2], b_ref[:, n * 512 : (n + 1) * 512], preferred_element_type=F32).astype(BF16)
             for m in range(2):
                 wide = jnp.concatenate(
                     [s[g * 256 : (g + 1) * 256, m * 256 : (m + 1) * 256] for g in range(GROUPS)], axis=1
                 )
                 cols = slice(n * 512 + m * 256, n * 512 + m * 256 + 256)
-                acc_ref[:, cols] += lax.dot_general(wide, w_ref[...], ANY_NT, preferred_element_type=F32)
-        return carry
-
-    lax.fori_loop(0, 32 // GROUPS, group, 0)
+                part = lax.dot_general(wide, w_ref[i % 2], ANY_NT, preferred_element_type=F32)
+                acc_ref[:, cols] = part if i == 0 else acc_ref[:, cols] + part
+
+    for i in range(32 // GROUPS):
+        group(i)
     for t in range(8):
         rows_ref[pl.ds(t, 256, stride=8), :] = acc_ref[:, t * 128 : (t + 1) * 128]
     out_ref[...] = rows_ref[...].astype(BF16).reshape(out_ref.shape)
@@ -235,8 +235,8 @@
         out_specs=vmem(1)[0],
         scratch_shapes=[
             pltpu.VMEM((128, 256), F32),
-            pltpu.VMEM((GROUPS * 256, 1024), BF16),
-            pltpu.VMEM((256, GROUPS * 256), BF16),
+            pltpu.VMEM((2, GROUPS * 256, 1024), BF16),
+            pltpu.VMEM((2, 256, GROUPS * 256), BF16),
             pltpu.VMEM((256, 1024), F32),
             pltpu.VMEM((2048, 128), F32),
         ],

time: 69.6 us -> 69.2 us (level)
  no operation moved by 1% of the time
where the time goes in v6:
time: 69.2 us; the launch traced here: 68.9 us
  Pallas kernels  33.4 us (48%)
  starting transfers between devices  20.4 us (29%)
  waiting for transfers between devices  14.3 us (21%)
  between operations  0.74 us (1%)
    pallas_call x1, Pallas kernels, make_sums(): pl.pallas_call(sum_kernel, out_shape=jax.ShapeDtypeStruct((128, 16, 128),...  23.1 us
    all_to_all x1, waiting for transfers between devices, local(): lax.all_to_all(sums, ('tm', 'det'), split_axis=0, concat_axis=0, tiled=True)  13.7 us
    all_to_all x1, starting transfers between devices, local(): lists = lax.all_to_all(own, 'det', split_axis=0, concat_axis=0, tiled=True)  8.04 us
    all_to_all x1, starting transfers between devices, local(): lax.all_to_all(sums, ('tm', 'det'), split_axis=0, concat_axis=0, tiled=True)  7.65 us
    pallas_call x1, Pallas kernels, make_filtered(): pl.pallas_call(filter_kernel, out_shape=(jax.ShapeDtypeStruct((1024, 1024...  7.01 us
    ppermute x1, starting transfers between devices, local(): low = lax.ppermute(last, 'tm', forward)  2.54 us
    ppermute x1, starting transfers between devices, local(): high = lax.ppermute(first, 'tm', backward)  2.2 us
    pallas_call x1, Pallas kernels, prepare(): pl.pallas_call(prepare_kernel, out_shape=(jax.ShapeDtypeStruct((32, 8, 12...  1.98 us
  transfers between devices with their start and end apart: 4, of which 2 were waited for; matrix products, arithmetic and copies ran while one was open for 0% of the time, Pallas kernels for 10%

profile of v6, /device:TPU:1, one launch (start us, length us, event | category | flops | bytes accessed | tf_op | source)
XLA Modules:
  0.0 68.9 jit_solution(13523449145753642325)
XLA Ops:
  0.0 0.0 copy-start.1
  0.7 2.0 %prepare.1 = (f32[32,8,128]{2,1,0:T(8,128)}, bf16[4,8,128]{2,1,0:T(8,128)(2,1)}, bf16[4,8,128]{2,1,0:T(8,128)(2,1)}) custom-call(s32[1,1]{1,0:T(1,128)} %bitcast.19.count_hbm, s32[8,128]{1,0:T(8,128)} %bitcast.26, s32[1,256]{1,0:T(1,128)} %bitcast.27, bf16[4,256,8,128]{3,2,1,0:T(8,128)(2,1)} %bitcast.23), custom_call_target="tpu_custom_call" | custom-call | flops 4000000 | bytes 200000 | tf_op jit(solution)/shard_map/prepare/pallas_call | solution.py:190
  2.6 2.5 %collective-permute-start = (bf16[4,8,128]{2,1,0:T(8,128)(2,1)}, bf16[4,8,128]{2,1,0:T(8,128)(2,1)S(1)}, u32[]{:S(2)}, u32[]{:S(2)}) collective-permute-start(bf16[4,8,128]{2,1,0:T(8,128)(2,1)} %get-tuple-element.11), channel_id=1, source_target_pairs={{0,32},{32,64},{64,96},{96,0},{1,33},{33,65},{65,97},{97,1},{2,34}... | collective-permute-start | bytes 24584 | tf_op jit(solution)/shard_map/ppermute | solution.py:271
  5.2 2.2 %collective-permute-start.1 = (bf16[4,8,128]{2,1,0:T(8,128)(2,1)}, bf16[4,8,128]{2,1,0:T(8,128)(2,1)S(1)}, u32[]{:S(2)}, u32[]{:S(2)}) collective-permute-start(bf16[4,8,128]{2,1,0:T(8,128)(2,1)} %get-tuple-element.12), channel_id=1, source_target_pairs={{32,0},{64,32},{96,64},{0,96},{33,1},{65,33},{97,65},{1,97},{34,2}... | collective-permute-start | bytes 24584 | tf_op jit(solution)/shard_map/ppermute | solution.py:272
  7.4 8.0 %all-to-all-start = ((f32[32,8,128]{2,1,0:T(8,128)}), f32[32,8,128]{2,1,0:T(8,128)S(1)}, u32[]{:S(2)}, u32[]{:S(2)}) async-start(f32[32,8,128]{2,1,0:T(8,128)} %get-tuple-element.10), calls=%async_computation | async-start | bytes 262144 | tf_op jit(solution)/shard_map/all_to_all | solution.py:273
  15.4 0.0 collective-permute-done.low_ref
  15.4 0.0 collective-permute-done.1.high_ref
  15.5 0.0 copy-done.1
  15.5 7.0 %make_filtered.1 = (bf16[1024,1024]{1,0:T(8,128)(2,1)S(1)}, bf16[1024,256]{1,0:T(8,128)(2,1)S(1)}) custom-call(bf16[4,256,8,128]{3,2,1,0:T(8,128)(2,1)} %bitcast.24, bf16[4,8,128]{2,1,0:T(8,128)(2,1)S(1)} %collective-permute-done.low_ref, bf16[4,8,128]{2,1,0:T(8,128)(2,1)S(1)} %collective-permute-done.1.high_ref, bf16[32,129]{1,0:T(8,128)(2,1)S(1)} %copy-done.1, ...), custom_call_target="tpu_custom_call" | custom-call | flops 5000000000 | bytes 7000000 | tf_op jit(solution)/shard_map/make_filtered/pallas_call | solution.py:209
  22.5 0.6 all-to-all-done
  23.1 0.0 copy-start.2
  23.1 0.0 copy-start
  23.1 23.1 %make_sums.1 = bf16[128,16,128]{2,1,0:T(8,128)(2,1)} custom-call(f32[256,128]{1,0:T(8,128)S(1)} %bitcast.20, bf16[1024,1024]{1,0:T(8,128)(2,1)S(1)} %get-tuple-element.13.b_ref, bf16[1024,256]{1,0:T(8,128)(2,1)S(1)} %get-tuple-element.14.rep_ref), custom_call_target="tpu_custom_call" | custom-call | flops 22000001024 | bytes 3000000 | tf_op jit(solution)/shard_map/make_sums/pallas_call | solution.py:231
  46.2 7.6 %all-to-all-start.1 = ((bf16[128,16,128]{2,1,0:T(8,128)(2,1)}), bf16[128,16,128]{2,1,0:T(8,128)(2,1)S(1)}, u32[]{:S(2)}, u32[]{:S(2)}) async-start(bf16[128,16,128]{2,1,0:T(8,128)(2,1)} %make_sums.1), calls=%async_computation.1 | async-start | bytes 1048576 | tf_op jit(solution)/shard_map/all_to_all | solution.py:276
  53.8 0.0 copy-done.2
  53.9 13.7 %all-to-all-done.1.in_ref = bf16[128,16,128]{2,1,0:T(8,128)(2,1)S(1)} async-done(((bf16[128,16,128]{2,1,0:T(8,128)(2,1)}), bf16[128,16,128]{2,1,0:T(8,128)(2,1)S(1)}, u32[]{:S(2)}, u32[]{:S(2)}) %all-to-all-start.1) | async-done | bytes 524320 | tf_op jit(solution)/shard_map/all_to_all | solution.py:276
  67.6 0.0 copy-done
  67.6 1.3 %make_tiles.1 = f32[256,128]{1,0:T(8,128)} custom-call(bf16[128,16,128]{2,1,0:T(8,128)(2,1)S(1)} %all-to-all-done.1.in_ref, f32[32,128]{1,0:T(8,128)S(1)} %bitcast.22, f32[32,128]{1,0:T(8,128)S(1)} %bitcast.21), custom_call_target="tpu_custom_call" | custom-call | flops 40000000 | bytes 700000 | tf_op jit(solution)/shard_map/make_tiles/pallas_call | solution.py:250
  (1 shorter events, 0.0 us)
Async XLA Ops:
  0.0 15.5 %copy-start.1 = (bf16[32,129]{1,0:T(8,128)(2,1)S(1)}, bf16[32,129]{1,0:T(8,128)(2,1)}, u32[]{:S(2)}) copy-start(bf16[32,129]{1,0:T(8,128)(2,1)} %taps_hbm.1) | copy-start | bytes 24772
  2.6 12.8 %collective-permute-start = (bf16[4,8,128]{2,1,0:T(8,128)(2,1)}, bf16[4,8,128]{2,1,0:T(8,128)(2,1)S(1)}, u32[]{:S(2)}, u32[]{:S(2)}) collective-permute-start(bf16[4,8,128]{2,1,0:T(8,128)(2,1)} %get-tuple-element.11), channel_id=1, source_target_pairs={{0,32},{32,64},{64,96},{96,0},{1,33},{33,65},{65,97},{97,1},{2,34}... | collective-permute-start | bytes 24584 | tf_op jit(solution)/shard_map/ppermute | solution.py:271
  5.2 10.3 %collective-permute-start.1 = (bf16[4,8,128]{2,1,0:T(8,128)(2,1)}, bf16[4,8,128]{2,1,0:T(8,128)(2,1)S(1)}, u32[]{:S(2)}, u32[]{:S(2)}) collective-permute-start(bf16[4,8,128]{2,1,0:T(8,128)(2,1)} %get-tuple-element.12), channel_id=1, source_target_pairs={{32,0},{64,32},{96,64},{0,96},{33,1},{65,33},{97,65},{1,97},{34,2}... | collective-permute-start | bytes 24584 | tf_op jit(solution)/shard_map/ppermute | solution.py:272
  7.4 15.7 %all-to-all-start = ((f32[32,8,128]{2,1,0:T(8,128)}), f32[32,8,128]{2,1,0:T(8,128)S(1)}, u32[]{:S(2)}, u32[]{:S(2)}) async-start(f32[32,8,128]{2,1,0:T(8,128)} %get-tuple-element.10), calls=%async_computation | async-start | bytes 262144 | tf_op jit(solution)/shard_map/all_to_all | solution.py:273
  23.1 30.8 %copy-start.2 = (f32[128,32]{0,1:T(8,128)S(1)}, f32[128,32]{0,1:T(8,128)}, u32[]{:S(2)}) copy-start(f32[128,32]{0,1:T(8,128)} %param.12) | copy-start | bytes 49156
  23.1 44.5 %copy-start = (f32[128,32]{0,1:T(8,128)S(1)}, f32[128,32]{0,1:T(8,128)}, u32[]{:S(2)}) copy-start(f32[128,32]{0,1:T(8,128)} %param.11) | copy-start | bytes 49156
  46.2 21.4 %all-to-all-start.1 = ((bf16[128,16,128]{2,1,0:T(8,128)(2,1)}), bf16[128,16,128]{2,1,0:T(8,128)(2,1)S(1)}, u32[]{:S(2)}, u32[]{:S(2)}) async-start(bf16[128,16,128]{2,1,0:T(8,128)(2,1)} %make_sums.1), calls=%async_computation.1 | async-start | bytes 1048576 | tf_op jit(solution)/shard_map/all_to_all | solution.py:276
